TPU v7x, 256 devices: a whole 4x4x8 slice. The times are simulated.
256 devices in a mesh: fsdp: 16 (over y_lo, z), ctx: 16 (over x, y_hi, core).
Axes of the slice: x: 4, y: 4 (y_hi: 2, y_lo: 2; y = y_hi * 2 + y_lo), z: 8, core: 2. Of those that a mesh axis runs over, the one named last changes fastest.
Arguments:
- query_rows: bfloat16 [16, 2048, 2560], P('fsdp', 'ctx'), may hold values from -6 to 6
- key_rows: bfloat16 [16, 2048, 2560], P('fsdp', 'ctx'), may hold values from -6.6 to 6.6
- value_rows: bfloat16 [16, 2048, 2560], P('fsdp', 'ctx'), may hold values from -6 to 6
- query_tangent: bfloat16 [16, 2048, 2560], P('fsdp', 'ctx'), may hold values from -6 to 6
- key_tangent: bfloat16 [16, 2048, 2560], P('fsdp', 'ctx'), may hold values from -6 to 6
- value_tangent: bfloat16 [16, 2048, 2560], P('fsdp', 'ctx'), may hold values from -6 to 6
- cotangent: bfloat16 [16, 2048, 2560], P('fsdp', 'ctx'), may hold values from -6 to 6
- out_weight: bfloat16 [2560, 2560], P('fsdp'), may hold values from -0.125 to 0.125
Outputs:
- tangent_out: bfloat16 [16, 2048, 2560], P('fsdp', 'ctx')
- query_grad: bfloat16 [16, 2048, 2560], P('fsdp', 'ctx')
- key_grad: bfloat16 [16, 2048, 2560], P('fsdp', 'ctx')
- value_grad: bfloat16 [16, 2048, 2560], P('fsdp', 'ctx')
All inputs are finite; a program needn't handle non-finite values.
Results may differ from a plain program's by a relative error of at most 0.0163.
Values may be sent and summed in bfloat16 or wider, within the bound.
No kernel may reach another device: no remote copies, remote signals or barrier semaphores. Data moves between devices by JAX's collectives and lax.ppermute only.
A program may use at most 128 MiB of HBM per device.

v0:
```python
import jax
import jax.numpy as jnp
from jax import lax
from jax.sharding import PartitionSpec as P

HEADS = 20
HEAD_DIM = 128


def from_behind(block, axis, distance):
    devices = range(lax.axis_size(axis))
    route = [((i - distance) % len(devices), i) for i in devices]
    return lax.ppermute(block, axis, route)


def attend(query_block, key_window, value_window, tq_block, tk_window, tv_window, grad_block):
    factor = HEAD_DIM ** (-0.5)
    rows = query_block.shape[0]
    span = key_window.shape[0]
    query_h = query_block.reshape(rows, HEADS, HEAD_DIM)
    key_h = key_window.reshape(span, HEADS, HEAD_DIM)
    value_h = value_window.reshape(span, HEADS, HEAD_DIM)
    tq_h = tq_block.reshape(rows, HEADS, HEAD_DIM)
    tk_h = tk_window.reshape(span, HEADS, HEAD_DIM)
    tv_h = tv_window.reshape(span, HEADS, HEAD_DIM)
    grad_h = grad_block.reshape(rows, HEADS, HEAD_DIM)
    scores = jnp.einsum("ihd,jhd->hij", query_h, key_h, preferred_element_type=jnp.float32) * factor
    top_score = jnp.max(scores, axis=-1, keepdims=True)
    expos = jnp.exp(scores - top_score)
    totals = jnp.sum(expos, axis=-1, keepdims=True)
    weights = expos / totals
    weights_b = weights.astype(jnp.bfloat16)
    attn = jnp.einsum("hij,jhd->ihd", weights_b, value_h, preferred_element_type=jnp.float32)
    tan_scores = (
        jnp.einsum("ihd,jhd->hij", tq_h, key_h, preferred_element_type=jnp.float32)
        + jnp.einsum("ihd,jhd->hij", query_h, tk_h, preferred_element_type=jnp.float32)
    ) * factor
    tan_prob = weights * (tan_scores - jnp.sum(weights * tan_scores, axis=-1, keepdims=True))
    tan_prob_b = tan_prob.astype(jnp.bfloat16)
    tan_attn = jnp.einsum(
        "hij,jhd->ihd", weights_b, tv_h, preferred_element_type=jnp.float32
    ) + jnp.einsum("hij,jhd->ihd", tan_prob_b, value_h, preferred_element_type=jnp.float32)
    tan_attn = tan_attn.reshape(rows, -1).astype(jnp.bfloat16)
    grad_prob = jnp.einsum("ihd,jhd->hij", grad_h, value_h, preferred_element_type=jnp.float32)
    delta = jnp.einsum("ihd,ihd->hi", grad_h.astype(jnp.float32), attn)[:, :, None]
    grad_scores = (weights * (grad_prob - delta) * factor).astype(jnp.bfloat16)
    query_grad = (
        jnp.einsum("hij,jhd->ihd", grad_scores, key_h, preferred_element_type=jnp.float32)
        .reshape(rows, -1)
        .astype(jnp.bfloat16)
    )
    key_terms = jnp.einsum(
        "hij,ihd->jhd", grad_scores, query_h, preferred_element_type=jnp.float32
    ).reshape(span, -1)
    value_terms = jnp.einsum(
        "hij,ihd->jhd", weights_b, grad_h, preferred_element_type=jnp.float32
    ).reshape(span, -1)
    return (tan_attn, query_grad, key_terms, value_terms, (top_score, totals, delta))


def body(
    query_rows,
    key_rows,
    value_rows,
    query_tangent,
    key_tangent,
    value_tangent,
    cotangent,
    out_weight,
):
    queries = query_rows[0]
    key_own = key_rows[0]
    value_own = value_rows[0]
    tq_own = query_tangent[0]
    tk_own = key_tangent[0]
    tv_own = value_tangent[0]
    grad_out = cotangent[0]
    rows = queries.shape[0]
    full_weight = lax.all_gather(out_weight, "fsdp", axis=0, tiled=True)
    near_blocks = from_behind((key_own, value_own, tk_own, tv_own), "ctx", 1)
    far_blocks = from_behind(
        (near_blocks[0], near_blocks[1], near_blocks[2], near_blocks[3]), "ctx", 1
    )
    key_window = jnp.concatenate([far_blocks[0], near_blocks[0], key_own], axis=0)
    value_window = jnp.concatenate([far_blocks[1], near_blocks[1], value_own], axis=0)
    tk_window = jnp.concatenate([far_blocks[2], near_blocks[2], tk_own], axis=0)
    tv_window = jnp.concatenate([far_blocks[3], near_blocks[3], tv_own], axis=0)
    grad_attn = jnp.einsum(
        "io,ao->ia", grad_out, full_weight, preferred_element_type=jnp.float32
    ).astype(jnp.bfloat16)
    tan_attn, query_grad, key_terms, value_terms, statistics = attend(
        queries, key_window, value_window, tq_own, tk_window, tv_window, grad_attn
    )
    tangent_out = jnp.dot(tan_attn, full_weight, preferred_element_type=jnp.float32).astype(
        jnp.bfloat16
    )
    back_near = from_behind((key_terms[rows : 2 * rows], value_terms[rows : 2 * rows]), "ctx", -1)
    back_far = from_behind((key_terms[:rows], value_terms[:rows]), "ctx", -2)
    key_grad = (key_terms[2 * rows :] + back_near[0] + back_far[0]).astype(jnp.bfloat16)
    value_grad = (value_terms[2 * rows :] + back_near[1] + back_far[1]).astype(jnp.bfloat16)
    return (tangent_out[None], query_grad[None], key_grad[None], value_grad[None])


def solution(mesh):
    return jax.shard_map(
        body,
        mesh=mesh,
        in_specs=(
            P("fsdp", "ctx", None),
            P("fsdp", "ctx", None),
            P("fsdp", "ctx", None),
            P("fsdp", "ctx", None),
            P("fsdp", "ctx", None),
            P("fsdp", "ctx", None),
            P("fsdp", "ctx", None),
            P("fsdp", None),
        ),
        out_specs=(
            P("fsdp", "ctx", None),
            P("fsdp", "ctx", None),
            P("fsdp", "ctx", None),
            P("fsdp", "ctx", None),
        ),
        check_vma=False,
    )
```

profile of v0, /device:TPU:1, one launch (start us, length us, event | category | flops | bytes accessed | tf_op | source)
XLA Modules:
  0.0 341.3 jit_solution(9249923809160908942)
XLA Ops:
  7.2 0.0 all-gather.2.cloned.1.call-start
  7.2 0.7 all-gather.2.cloned.1.call-update
  7.9 1.4 copy.42
  9.3 4.4 %collective-permute-start.2 = (bf16[128,2560]{0,1:T(8,128)(2,1)S(1)}, bf16[128,2560]{0,1:T(8,128)(2,1)}, u32[]{:S(2)}, u32[]{:S(2)}) collective-permute-start(bf16[128,2560]{0,1:T(8,128)(2,1)S(1)} %bitcast.99), channel_id=1, source_target_pairs={{15,0},{0,1},{1,2},{2,3},{3,4},{4,5},{5,6},{6,7},{7,8},{8,9},{9,10... | collective-permute-start | bytes 1966088 | tf_op jit(solution)/shard_map/ppermute | solution.py:13
  13.7 1.4 copy.55
  15.1 0.1 collective-permute-start.6
  15.2 1.4 collective-permute-start.4
  16.6 0.1 collective-permute-start
  16.7 4.6 %collective-permute-done.2 = bf16[128,2560]{0,1:T(8,128)(2,1)} collective-permute-done((bf16[128,2560]{0,1:T(8,128)(2,1)S(1)}, bf16[128,2560]{0,1:T(8,128)(2,1)}, u32[]{:S(2)}, u32[]{:S(2)}) %collective-permute-start.2) | collective-permute-done | bytes 655392 | tf_op jit(solution)/shard_map/ppermute | solution.py:13
  21.3 4.1 %collective-permute-start.3 = (bf16[128,2560]{0,1:T(8,128)(2,1)}, bf16[128,2560]{0,1:T(8,128)(2,1)}, u32[]{:S(2)}, u32[]{:S(2)}) collective-permute-start(bf16[128,2560]{0,1:T(8,128)(2,1)} %collective-permute-done.2), channel_id=1, source_target_pairs={{15,0},{0,1},{1,2},{2,3},{3,4},{4,5},{5,6},{6,7},{7,8},{8,9},{9,10... | collective-permute-start | bytes 1966088 | tf_op jit(solution)/shard_map/ppermute | solution.py:13
  25.3 134.6 %collective-permute-done.6 = bf16[128,2560]{0,1:T(8,128)(2,1)} collective-permute-done((bf16[128,2560]{0,1:T(8,128)(2,1)S(1)}, bf16[128,2560]{0,1:T(8,128)(2,1)}, u32[]{:S(2)}, u32[]{:S(2)}) %collective-permute-start.6) | collective-permute-done | bytes 655392 | tf_op jit(solution)/shard_map/ppermute | solution.py:13
  159.9 4.1 %collective-permute-start.7 = (bf16[128,2560]{0,1:T(8,128)(2,1)}, bf16[128,2560]{0,1:T(8,128)(2,1)}, u32[]{:S(2)}, u32[]{:S(2)}) collective-permute-start(bf16[128,2560]{0,1:T(8,128)(2,1)} %collective-permute-done.6), channel_id=1, source_target_pairs={{15,0},{0,1},{1,2},{2,3},{3,4},{4,5},{5,6},{6,7},{7,8},{8,9},{9,10... | collective-permute-start | bytes 1966088 | tf_op jit(solution)/shard_map/ppermute | solution.py:13
  164.0 3.0 collective-permute-done.4
  167.1 4.0 %collective-permute-start.5 = (bf16[128,2560]{1,0:T(8,128)(2,1)}, bf16[128,2560]{1,0:T(8,128)(2,1)}, u32[]{:S(2)}, u32[]{:S(2)}) collective-permute-start(bf16[128,2560]{1,0:T(8,128)(2,1)} %collective-permute-done.4), channel_id=1, source_target_pairs={{15,0},{0,1},{1,2},{2,3},{3,4},{4,5},{5,6},{6,7},{7,8},{8,9},{9,10... | collective-permute-start | bytes 1966088 | tf_op jit(solution)/shard_map/ppermute | solution.py:13
  171.1 3.0 collective-permute-done
  174.1 4.0 %collective-permute-start.1 = (bf16[128,2560]{1,0:T(8,128)(2,1)}, bf16[128,2560]{1,0:T(8,128)(2,1)}, u32[]{:S(2)}, u32[]{:S(2)}) collective-permute-start(bf16[128,2560]{1,0:T(8,128)(2,1)} %collective-permute-done), channel_id=1, source_target_pairs={{15,0},{0,1},{1,2},{2,3},{3,4},{4,5},{5,6},{6,7},{7,8},{8,9},{9,10... | collective-permute-start | bytes 1966088 | tf_op jit(solution)/shard_map/ppermute | solution.py:13
  178.1 2.2 copy.52
  180.3 1.1 copy.41
  181.4 1.4 copy.47
  182.8 0.3 copy.46
  183.1 2.4 copy.53
  185.5 1.1 copy.59
  186.6 1.4 copy.45
  188.1 2.4 copy.58
  190.5 2.2 copy.51
  192.6 2.2 copy.40
  194.8 1.4 copy.44
  196.2 2.4 copy.57
  198.6 2.2 copy.50
  200.8 1.4 collective-permute-done.1
  202.2 2.2 copy.39
  204.4 3.6 %fusion.44 = f32[20,384,128]{2,1,0:T(8,128)} fusion(bf16[128,20,128]{0,2,1:T(8,128)(2,1)} %bitcast.98, bf16[128,20,128]{2,0,1:T(8,128)(2,1)S(1)} %copy.46, bf16[128,20,128]{2,0,1:T(8,128)(2,1)S(1)} %copy.45, bf16[128,20,128]{2,0,1:T(8,128)(2,1)S(1)} %copy.44), kind=kOutput, calls=%fused_computation.53 | convolution fusion | flops 257556480 | bytes 6553600 | tf_op jit(solution)/shard_map/ihd,jhd->hij/dot_general | solution.py:35
  208.0 3.2 fusion.47
  211.2 4.9 %fusion.1 = (f32[20,128]{1,0:T(8,128)S(1)}, f32[20,384,128]{2,1,0:T(8,128)S(1)}) fusion(f32[20,128,384]{1,2,0:T(8,128)} %get-tuple-element.19, f32[20,128]{1,0:T(8,128)S(1)} %get-tuple-element.18, f32[20,384,128]{2,1,0:T(8,128)} %fusion.44, bf16[128,20,128]{0,2,1:T(8,128)(2,1)S(1)} %bitcast.96, bf16[128,20,128]{2,0,1:T(8,128)(2,1)} %copy.59, ...), kind=kOutput, calls=%fused_computation.3 | convolution fusion | flops 262469120 | bytes 14438400 | tf_op jit(solution)/shard_map/ihd,jhd->hij/dot_general | solution.py:36
  216.1 0.7 copy-done.17
  216.8 1.0 fusion.10
  217.8 0.1 copy-done.10
  217.9 0.2 copy-done.11
  218.1 0.2 copy-done.14
  218.3 1.6 fusion.29
  219.9 9.0 %convolution_convert_fusion = bf16[128,2560]{1,0:T(8,128)(2,1)S(1)} fusion(bf16[2560,2560]{1,0:T(8,128)(2,1)} %all-gather.2.cloned.1.call-done, bf16[1,128,2560]{2,1,0:T(8,128)(2,1)S(1)} %copy-done), kind=kOutput, calls=%fused_computation.12 | convolution fusion | flops 1678049280 | bytes 14417920 | tf_op jit(solution)/shard_map/io,ao->ia/dot_general | solution.py:88
  228.9 0.3 copy.62
  229.2 3.3 fusion.32
  232.5 0.4 copy-done.18
  232.9 4.0 %convolution_bitcast_fusion = f32[384,20,128]{0,2,1:T(8,128)} fusion(bf16[128,20,128]{0,2,1:T(8,128)(2,1)} %bitcast.119, f32[20,128,384]{1,2,0:T(8,128)S(1)} %copy-done.18, f32[20,128]{1,0:T(8,128)S(1)} %get-tuple-element.18), kind=kOutput, calls=%fused_computation.16 | convolution fusion | flops 253624320 | bytes 8529920 | tf_op jit(solution)/shard_map/hij,ihd->jhd/dot_general | solution.py:55
  237.0 1.3 multiply_convert_fusion
  238.2 0.9 convolution_bitcast_fusion.1
  239.2 1.6 fusion.46
  240.8 2.9 copy.71
  243.6 1.5 copy.69
  245.1 6.6 %collective-permute-start.8 = (f32[128,2560]{1,0:T(8,128)}, f32[128,2560]{1,0:T(8,128)}, u32[]{:S(2)}, u32[]{:S(2)}) collective-permute-start(f32[128,2560]{1,0:T(8,128)} %copy.69), channel_id=1, source_target_pairs={{1,0},{2,1},{3,2},{4,3},{5,4},{6,5},{7,6},{8,7},{9,8},{10,9},{11,1... | collective-permute-start | bytes 3932168 | tf_op jit(solution)/shard_map/ppermute | solution.py:13
  251.7 2.7 convolution_convert_fusion.2
  254.4 1.1 copy.76
  255.5 0.4 copy.70
  255.9 4.1 %fusion.45 = (f32[128,20,128]{0,2,1:T(8,128)}, f32[128,20,128]{0,2,1:T(8,128)S(1)}, f32[128,20,128]{0,2,1:T(8,128)}) fusion(f32[384,20,128]{0,2,1:T(8,128)} %convolution_bitcast_fusion), kind=kLoop, calls=%fused_computation.54 | loop fusion | bytes 7864320 | tf_op jit(solution)/shard_map/slice | solution.py:97
  260.0 1.5 copy.75
  261.5 1.7 copy.74
  263.2 2.8 copy.73
  266.0 7.7 %fusion.6 = bf16[1,128,2560]{2,1,0:T(8,128)(2,1)} fusion(bf16[128,2560]{0,1:T(8,128)(2,1)} %bitcast.103, bf16[2560,2560]{1,0:T(8,128)(2,1)} %all-gather.2.cloned.1.call-done), kind=kOutput, calls=%fused_computation.14 | convolution fusion | flops 1678049280 | bytes 14417920 | tf_op jit(solution)/shard_map/dot_general | solution.py:94
  273.8 1.1 collective-permute-done.9
  274.9 29.2 %collective-permute-done.8 = f32[128,2560]{1,0:T(8,128)} collective-permute-done((f32[128,2560]{1,0:T(8,128)}, f32[128,2560]{1,0:T(8,128)}, u32[]{:S(2)}, u32[]{:S(2)}) %collective-permute-start.8) | collective-permute-done | bytes 1310752 | tf_op jit(solution)/shard_map/ppermute | solution.py:13
  304.0 2.8 fusion.33
  306.8 25.2 %collective-permute-done.10 = f32[128,2560]{1,0:T(8,128)S(1)} collective-permute-done((f32[128,2560]{1,0:T(8,128)}, f32[128,2560]{1,0:T(8,128)S(1)}, u32[]{:S(2)}, u32[]{:S(2)}) %collective-permute-start.10) | collective-permute-done | bytes 1310752 | tf_op jit(solution)/shard_map/ppermute | solution.py:13
  332.0 2.4 fusion.34
  (41 shorter events, 0.1 us)
Async XLA Ops:
  7.2 212.7 %copy-start = (bf16[1,128,2560]{2,1,0:T(8,128)(2,1)S(1)}, bf16[1,128,2560]{2,1,0:T(8,128)(2,1)}, u32[]{:S(2)}) copy-start(bf16[1,128,2560]{2,1,0:T(8,128)(2,1)} %param.14) | copy-start | bytes 1966084
  7.2 173.1 %copy-start.7 = (bf16[1,128,2560]{2,1,0:T(8,128)(2,1)S(1)}, bf16[1,128,2560]{2,1,0:T(8,128)(2,1)}, u32[]{:S(2)}) copy-start(bf16[1,128,2560]{2,1,0:T(8,128)(2,1)} %param.13) | copy-start | bytes 1966084
  7.2 212.7 %all-gather.2.cloned.1.call-start = ((), (), s32[]{:S(2)}) async-start(), calls=%async_computation | async-start | bytes 13926400 | tf_op jit(solution)/shard_map/all_gather | solution.py:79
  9.3 11.9 %collective-permute-start.2 = (bf16[128,2560]{0,1:T(8,128)(2,1)S(1)}, bf16[128,2560]{0,1:T(8,128)(2,1)}, u32[]{:S(2)}, u32[]{:S(2)}) collective-permute-start(bf16[128,2560]{0,1:T(8,128)(2,1)S(1)} %bitcast.99), channel_id=1, source_target_pairs={{15,0},{0,1},{1,2},{2,3},{3,4},{4,5},{5,6},{6,7},{7,8},{8,9},{9,10... | collective-permute-start | bytes 1966088 | tf_op jit(solution)/shard_map/ppermute | solution.py:13
  15.1 144.8 %collective-permute-start.6 = (bf16[128,2560]{0,1:T(8,128)(2,1)S(1)}, bf16[128,2560]{0,1:T(8,128)(2,1)}, u32[]{:S(2)}, u32[]{:S(2)}) collective-permute-start(bf16[128,2560]{0,1:T(8,128)(2,1)S(1)} %bitcast.101), channel_id=1, source_target_pairs={{15,0},{0,1},{1,2},{2,3},{3,4},{4,5},{5,6},{6,7},{7,8},{8,9},{9,10... | collective-permute-start | bytes 1966088 | tf_op jit(solution)/shard_map/ppermute | solution.py:13
  15.2 151.8 %collective-permute-start.4 = (bf16[128,2560]{1,0:T(8,128)(2,1)}, bf16[128,2560]{1,0:T(8,128)(2,1)}, u32[]{:S(2)}, u32[]{:S(2)}) collective-permute-start(bf16[128,2560]{1,0:T(8,128)(2,1)} %bitcast.104), channel_id=1, source_target_pairs={{15,0},{0,1},{1,2},{2,3},{3,4},{4,5},{5,6},{6,7},{7,8},{8,9},{9,10... | collective-permute-start | bytes 1966088 | tf_op jit(solution)/shard_map/ppermute | solution.py:13
  16.6 157.5 %collective-permute-start = (bf16[128,2560]{1,0:T(8,128)(2,1)}, bf16[128,2560]{1,0:T(8,128)(2,1)}, u32[]{:S(2)}, u32[]{:S(2)}) collective-permute-start(bf16[128,2560]{1,0:T(8,128)(2,1)} %bitcast.105), channel_id=1, source_target_pairs={{15,0},{0,1},{1,2},{2,3},{3,4},{4,5},{5,6},{6,7},{7,8},{8,9},{9,10... | collective-permute-start | bytes 1966088 | tf_op jit(solution)/shard_map/ppermute | solution.py:13
  21.3 173.5 %collective-permute-start.3 = (bf16[128,2560]{0,1:T(8,128)(2,1)}, bf16[128,2560]{0,1:T(8,128)(2,1)}, u32[]{:S(2)}, u32[]{:S(2)}) collective-permute-start(bf16[128,2560]{0,1:T(8,128)(2,1)} %collective-permute-done.2), channel_id=1, source_target_pairs={{15,0},{0,1},{1,2},{2,3},{3,4},{4,5},{5,6},{6,7},{7,8},{8,9},{9,10... | collective-permute-start | bytes 1966088 | tf_op jit(solution)/shard_map/ppermute | solution.py:13
  159.9 36.3 %collective-permute-start.7 = (bf16[128,2560]{0,1:T(8,128)(2,1)}, bf16[128,2560]{0,1:T(8,128)(2,1)}, u32[]{:S(2)}, u32[]{:S(2)}) collective-permute-start(bf16[128,2560]{0,1:T(8,128)(2,1)} %collective-permute-done.6), channel_id=1, source_target_pairs={{15,0},{0,1},{1,2},{2,3},{3,4},{4,5},{5,6},{6,7},{7,8},{8,9},{9,10... | collective-permute-start | bytes 1966088 | tf_op jit(solution)/shard_map/ppermute | solution.py:13
  167.1 31.6 %collective-permute-start.5 = (bf16[128,2560]{1,0:T(8,128)(2,1)}, bf16[128,2560]{1,0:T(8,128)(2,1)}, u32[]{:S(2)}, u32[]{:S(2)}) collective-permute-start(bf16[128,2560]{1,0:T(8,128)(2,1)} %collective-permute-done.4), channel_id=1, source_target_pairs={{15,0},{0,1},{1,2},{2,3},{3,4},{4,5},{5,6},{6,7},{7,8},{8,9},{9,10... | collective-permute-start | bytes 1966088 | tf_op jit(solution)/shard_map/ppermute | solution.py:13
  174.1 28.1 %collective-permute-start.1 = (bf16[128,2560]{1,0:T(8,128)(2,1)}, bf16[128,2560]{1,0:T(8,128)(2,1)}, u32[]{:S(2)}, u32[]{:S(2)}) collective-permute-start(bf16[128,2560]{1,0:T(8,128)(2,1)} %collective-permute-done), channel_id=1, source_target_pairs={{15,0},{0,1},{1,2},{2,3},{3,4},{4,5},{5,6},{6,7},{7,8},{8,9},{9,10... | collective-permute-start | bytes 1966088 | tf_op jit(solution)/shard_map/ppermute | solution.py:13
  183.1 24.8 %copy-start.2 = (bf16[128,20,128]{2,0,1:T(8,128)(2,1)}, bf16[128,20,128]{2,0,1:T(8,128)(2,1)S(1)}, u32[]{:S(2)}) copy-start(bf16[128,20,128]{2,0,1:T(8,128)(2,1)S(1)} %copy.46) | copy-start | bytes 1966084
  188.0 19.9 %copy-start.4 = (bf16[128,20,128]{2,0,1:T(8,128)(2,1)}, bf16[128,20,128]{2,0,1:T(8,128)(2,1)S(1)}, u32[]{:S(2)}) copy-start(bf16[128,20,128]{2,0,1:T(8,128)(2,1)S(1)} %copy.45) | copy-start | bytes 1966084
  196.2 11.8 %copy-start.5 = (bf16[128,20,128]{2,0,1:T(8,128)(2,1)}, bf16[128,20,128]{2,0,1:T(8,128)(2,1)S(1)}, u32[]{:S(2)}) copy-start(bf16[128,20,128]{2,0,1:T(8,128)(2,1)S(1)} %copy.44) | copy-start | bytes 1966084
  211.2 4.9 %copy-start.8 = (bf16[1,128,2560]{1,2,0:T(8,128)(2,1)S(1)}, bf16[1,128,2560]{1,2,0:T(8,128)(2,1)}, u32[]{:S(2)}) copy-start(bf16[1,128,2560]{1,2,0:T(8,128)(2,1)} %copy.52) | copy-start | bytes 1966084
  211.2 4.9 %copy-start.9 = (bf16[128,2560]{0,1:T(8,128)(2,1)S(1)}, bf16[128,2560]{0,1:T(8,128)(2,1)}, u32[]{:S(2)}) copy-start(bf16[128,2560]{0,1:T(8,128)(2,1)} %copy.51) | copy-start | bytes 1966084
  211.2 4.9 %copy-start.12 = (bf16[128,2560]{0,1:T(8,128)(2,1)S(1)}, bf16[128,2560]{0,1:T(8,128)(2,1)}, u32[]{:S(2)}) copy-start(bf16[128,2560]{0,1:T(8,128)(2,1)} %copy.50) | copy-start | bytes 1966084
  211.2 5.6 %copy-start.17 = (f32[20,128,384]{1,2,0:T(8,128)S(1)}, f32[20,128,384]{1,2,0:T(8,128)}, u32[]{:S(2)}) copy-start(f32[20,128,384]{1,2,0:T(8,128)} %get-tuple-element.19) | copy-start | bytes 11796484
  216.8 1.1 copy-start.10
  216.8 1.3 copy-start.11
  216.8 1.5 copy-start.14
  229.2 3.3 copy-start.15
  229.2 3.7 %copy-start.18 = (f32[20,128,384]{1,2,0:T(8,128)S(1)}, f32[20,128,384]{1,2,0:T(8,128)}, u32[]{:S(2)}) copy-start(f32[20,128,384]{1,2,0:T(8,128)} %get-tuple-element.19) | copy-start | bytes 11796484
  232.9 4.0 %copy-start.13 = (bf16[128,2560]{0,1:T(8,128)(2,1)S(1)}, bf16[128,2560]{0,1:T(8,128)(2,1)}, u32[]{:S(2)}) copy-start(bf16[128,2560]{0,1:T(8,128)(2,1)} %copy.50) | copy-start | bytes 1966084
  232.9 4.0 %copy-start.16 = (bf16[128,2560]{0,1:T(8,128)(2,1)S(1)}, bf16[128,2560]{0,1:T(8,128)(2,1)}, u32[]{:S(2)}) copy-start(bf16[128,2560]{0,1:T(8,128)(2,1)} %copy-done.15) | copy-start | bytes 1966084
  238.2 2.5 copy-start.6
  240.7 10.9 %copy-start.3 = (bf16[128,20,128]{2,0,1:T(8,128)(2,1)S(1)}, bf16[128,20,128]{2,0,1:T(8,128)(2,1)}, u32[]{:S(2)}) copy-start(bf16[128,20,128]{2,0,1:T(8,128)(2,1)} %copy-done.2) | copy-start | bytes 1966084
  243.6 31.3 %collective-permute-start.9 = (f32[128,2560]{1,0:T(8,128)}, f32[128,2560]{1,0:T(8,128)}, u32[]{:S(2)}, u32[]{:S(2)}) collective-permute-start(f32[128,2560]{1,0:T(8,128)} %copy.71), channel_id=1, source_target_pairs={{2,0},{3,1},{4,2},{5,3},{6,4},{7,5},{8,6},{9,7},{10,8},{11,9},{12,... | collective-permute-start | bytes 3932168 | tf_op jit(solution)/shard_map/ppermute | solution.py:13
  245.1 58.9 %collective-permute-start.8 = (f32[128,2560]{1,0:T(8,128)}, f32[128,2560]{1,0:T(8,128)}, u32[]{:S(2)}, u32[]{:S(2)}) collective-permute-start(f32[128,2560]{1,0:T(8,128)} %copy.69), channel_id=1, source_target_pairs={{1,0},{2,1},{3,2},{4,3},{5,4},{6,5},{7,6},{8,7},{9,8},{10,9},{11,1... | collective-permute-start | bytes 3932168 | tf_op jit(solution)/shard_map/ppermute | solution.py:13
  261.5 45.3 %collective-permute-start.11 = (f32[128,2560]{1,0:T(8,128)}, f32[128,2560]{1,0:T(8,128)}, u32[]{:S(2)}, u32[]{:S(2)}) collective-permute-start(f32[128,2560]{1,0:T(8,128)} %copy.75), channel_id=1, source_target_pairs={{2,0},{3,1},{4,2},{5,3},{6,4},{7,5},{8,6},{9,7},{10,8},{11,9},{12,... | collective-permute-start | bytes 3932168 | tf_op jit(solution)/shard_map/ppermute | solution.py:13
  266.0 66.0 %collective-permute-start.10 = (f32[128,2560]{1,0:T(8,128)}, f32[128,2560]{1,0:T(8,128)S(1)}, u32[]{:S(2)}, u32[]{:S(2)}) collective-permute-start(f32[128,2560]{1,0:T(8,128)} %copy.73), channel_id=1, source_target_pairs={{1,0},{2,1},{3,2},{4,3},{5,4},{6,5},{7,6},{8,7},{9,8},{10,9},{11,1... | collective-permute-start | bytes 3932168 | tf_op jit(solution)/shard_map/ppermute | solution.py:13
  266.0 68.4 %copy-start.1 = (bf16[1,128,2560]{2,1,0:T(8,128)(2,1)S(1)}, bf16[1,128,2560]{2,1,0:T(8,128)(2,1)}, u32[]{:S(2)}) copy-start(bf16[1,128,2560]{2,1,0:T(8,128)(2,1)} %param.14) | copy-start | bytes 1966084
Sparse Core Ops, SparseCore 0:
  9.8 152.2 all-gather.1
where the time goes:
time: 342 us; the launch traced here: 341 us
  waiting for transfers between devices  203 us (59%)
  local copies, waits for them, and re-layouts  47.1 us (14%)
  matrix products  43.2 us (13%)
  starting transfers between devices  28.7 us (8%)
  between operations  14.3 us (4%)
  other arithmetic  5.18 us (2%)
    ppermute x12, waiting for transfers between devices, from_behind(): return lax.ppermute(block, axis, route)  202 us
    ppermute x12, starting transfers between devices, from_behind(): return lax.ppermute(block, axis, route)  28.7 us
    unnamed x45, local copies, waits for them, and re-layouts  12.6 us
    dot_general x1, matrix products, body(): jnp.einsum('io,ao->ia', grad_out, full_weight, preferred_element_type=jnp...  8.98 us
    ppermute x4, local copies, waits for them, and re-layouts, from_behind(): return lax.ppermute(block, axis, route)  8.69 us
    dot_general x1, matrix products, body(): jnp.dot(tan_attn, full_weight, preferred_element_type=jnp.float32)  7.72 us
    slice x2, local copies, waits for them, and re-layouts, body(): value_terms[rows:2 * rows]  6.92 us
  transfers between devices with their start and end apart: 13, of which 8 were waited for; matrix products, arithmetic and copies ran while one was open for 20% of the time, Pallas kernels for 0%

commit v1 on v0

v1 whole, which is shorter than its diff:
```python
import functools

import jax
import jax.numpy as jnp
from jax import lax
from jax.experimental import pallas as pl
from jax.experimental.pallas import tpu as pltpu
from jax.sharding import Mesh
from jax.sharding import PartitionSpec as P

HEADS = 20
HEAD_DIM = 128
ROWS = 128
WIDTH = HEADS * HEAD_DIM
HALF = WIDTH // 2
HALF_HEADS = HEADS // 2
FACTOR = HEAD_DIM ** (-0.5)

AXES = ("yl", "z", "x", "yh", "c")
SIZES = (2, 8, 4, 2, 2)

F32 = jnp.float32
BF16 = jnp.bfloat16
VMEM_LIMIT = 48 * 1024 * 1024


def permute(block, move):
    route = []
    for index in range(256):
        rest, place = index, []
        for size in reversed(SIZES):
            place.append(rest % size)
            rest //= size
        goal = 0
        for coordinate, size in zip(move(*reversed(place)), SIZES):
            goal = goal * size + coordinate
        route.append((index, goal))
    return lax.ppermute(block, AXES, route)


def to_chip(step, cross=False):
    def move(yl, z, x, yh, c):
        chip = (x * 2 + yh + step) % 8
        return yl, z, chip // 2, chip % 2, (1 - c if cross else c)

    return move


def to_sibling(yl, z, x, yh, c):
    return yl, z, x, yh, 1 - c


def swap_low_and_core(yl, z, x, yh, c):
    return c, z, x, yh, yl


def pack_kernel(core, q, tq, k, tk, v, tv, cot, own_kv, sib_kv, sib_q, sems):
    c = core[0]
    mine = pl.multiple_of(c * HALF, HALF)
    other = pl.multiple_of((1 - c) * HALF, HALF)
    copies = []

    def put(source, start, target, entry):
        copy = pltpu.make_async_copy(
            source.at[0, :, pl.ds(start, HALF)], target.at[entry], sems.at[len(copies)]
        )
        copy.start()
        copies.append(copy)

    for entry, source in enumerate((k, tk, v, tv)):
        put(source, mine, own_kv, entry)
    for entry, source in enumerate((k, tk, v, tv)):
        put(source, other, sib_kv, entry)
    for entry, source in enumerate((q, tq)):
        put(source, other, sib_q, entry)
    put(cot, 0, sib_q, 2)
    put(cot, HALF, sib_q, 3)
    for copy in copies:
        copy.wait()


def pack(core, arrays):
    anywhere = pl.BlockSpec(memory_space=pl.ANY)
    four = jax.ShapeDtypeStruct((4, ROWS, HALF), BF16)
    return pl.pallas_call(
        pack_kernel,
        out_shape=(four, four, four),
        in_specs=[pl.BlockSpec(memory_space=pltpu.SMEM)] + [anywhere] * 7,
        out_specs=(anywhere, anywhere, anywhere),
        scratch_shapes=[pltpu.SemaphoreType.DMA((12,))],
        name="pack",
    )(core, *arrays)


def project_kernel(cot, sib_q, weight, out, both):
    @pl.when(pl.program_id(0) == 0)
    def _():
        both[:ROWS, :] = cot[0]
        both[ROWS:, :HALF] = sib_q[0]
        both[ROWS:, HALF:] = sib_q[1]

    out[...] = lax.dot_general(
        both[...], weight[...], (((1,), (1,)), ((), ())), preferred_element_type=F32
    ).astype(BF16)


def project(cot, sib_q, weight):
    tile = 256
    return pl.pallas_call(
        project_kernel,
        grid=(HALF // tile,),
        out_shape=jax.ShapeDtypeStruct((2 * ROWS, HALF), BF16),
        in_specs=[
            pl.BlockSpec((1, ROWS, WIDTH), lambda i: (0, 0, 0)),
            pl.BlockSpec((2, ROWS, HALF), lambda i: (1, 0, 0)),
            pl.BlockSpec((tile, WIDTH), lambda i: (i, 0)),
        ],
        out_specs=pl.BlockSpec((2 * ROWS, tile), lambda i: (0, i)),
        scratch_shapes=[pltpu.VMEM((2 * ROWS, WIDTH), BF16)],
        compiler_params=pltpu.CompilerParams(vmem_limit_bytes=VMEM_LIMIT),
        name="project",
    )(cot, sib_q, weight)


def dot(a, b, dims):
    return lax.dot_general(a, b, (dims, ((), ())), preferred_element_type=F32)


NT = ((1,), (1,))
NN = ((1,), (0,))
TN = ((0,), (0,))


def attend_kernel(
    core, q, tq, k, tk, v, tv, sib_kv, sib_q, far_own, far_sib, grad,
    tan_out, own_out, sib_out, back_own, back_sib,
    keys, values, tvals, queries, grads, prob_all, gs_all, tan_all, qg_all, kg_all, vg_all,
):
    c = core[0]
    mine = pl.multiple_of(c * ROWS, ROWS)
    other = pl.multiple_of((1 - c) * ROWS, ROWS)
    span = 3 * ROWS

    @pl.when(pl.program_id(0) == 0)
    def _():
        zero = jnp.zeros((ROWS, ROWS), BF16)
        for ref in (prob_all, gs_all):
            ref[:ROWS, span:] = zero
            ref[ROWS:, :ROWS] = zero

    def place(start, k_new, tk_new, v_new, tv_new):
        rows = pl.ds(start, ROWS)
        keys[rows, :HEAD_DIM] = k_new
        keys[rows, HEAD_DIM:] = tk_new
        values[rows, :] = v_new
        tvals[rows, :] = tv_new

    place(mine, *(far_own[i] for i in range(4)))
    place(other, *(far_sib[i] for i in range(4)))
    place(2 * ROWS + mine, k[0], tk[0], v[0], tv[0])
    place(2 * ROWS + other, *(sib_kv[i] for i in range(4)))
    queries[pl.ds(mine, ROWS), :HEAD_DIM] = tq[0]
    queries[pl.ds(mine, ROWS), HEAD_DIM:] = q[0]
    queries[pl.ds(other, ROWS), :HEAD_DIM] = sib_q[1]
    queries[pl.ds(other, ROWS), HEAD_DIM:] = sib_q[0]
    grads[pl.ds(mine, ROWS), :] = grad[:ROWS]
    grads[pl.ds(other, ROWS), :] = grad[ROWS:]

    for block in range(2):
        rows = slice(block * ROWS, (block + 1) * ROWS)
        seen = slice(block * ROWS, block * ROWS + span)
        query = queries[rows, :]
        key = keys[seen, :]
        value = values[seen, :]
        scores = dot(query[:, HEAD_DIM:], key[:, :HEAD_DIM], NT) * FACTOR
        tan_scores = dot(query, key, NT) * FACTOR
        grad_prob = dot(grads[rows, :], value, NT)
        top = jnp.max(scores, axis=-1, keepdims=True)
        expos = jnp.exp(scores - top)
        prob = expos * (1.0 / jnp.sum(expos, axis=-1, keepdims=True))
        prob_b = prob.astype(BF16)
        mean = jnp.sum(prob * tan_scores, axis=-1, keepdims=True)
        tan_prob = (prob * (tan_scores - mean)).astype(BF16)
        delta = jnp.sum(prob_b.astype(F32) * grad_prob, axis=-1, keepdims=True)
        gs = (prob * (grad_prob - delta) * FACTOR).astype(BF16)
        tan = dot(prob_b, tvals[seen, :], NN) + dot(tan_prob, value, NN)
        tan_all[rows, :] = tan.astype(BF16)
        qg_all[rows, :] = dot(gs, key[:, :HEAD_DIM], NN)
        prob_all[rows, seen] = prob_b
        gs_all[rows, seen] = gs

    kg_all[...] = dot(gs_all[...], queries[:, HEAD_DIM:], TN)
    vg_all[...] = dot(prob_all[...], grads[...], TN)

    my_rows, other_rows = pl.ds(mine, ROWS), pl.ds(other, ROWS)
    tan_out[:ROWS] = tan_all[my_rows, :]
    tan_out[ROWS:] = tan_all[other_rows, :]
    back_own[0] = kg_all[my_rows, :].astype(BF16)
    back_own[1] = vg_all[my_rows, :].astype(BF16)
    back_sib[0] = kg_all[other_rows, :].astype(BF16)
    back_sib[1] = vg_all[other_rows, :].astype(BF16)
    my_keys, other_keys = pl.ds(2 * ROWS + mine, ROWS), pl.ds(2 * ROWS + other, ROWS)
    own_out[0] = qg_all[my_rows, :]
    own_out[1] = kg_all[my_keys, :]
    own_out[2] = vg_all[my_keys, :]
    sib_out[0] = qg_all[other_rows, :].astype(BF16)
    sib_out[1] = kg_all[other_keys, :].astype(BF16)
    sib_out[2] = vg_all[other_keys, :].astype(BF16)


def attend(core, arrays, sib_kv, sib_q, far_own, far_sib, grad):
    raw = pl.BlockSpec((1, ROWS, HEAD_DIM), lambda h, core: (0, 0, core[0] * HALF_HEADS + h))

    def stack(n):
        return pl.BlockSpec((n, ROWS, HEAD_DIM), lambda h, core: (0, 0, h))

    two = pl.BlockSpec((2 * ROWS, HEAD_DIM), lambda h, core: (0, h))

    def out(n, dtype):
        return jax.ShapeDtypeStruct((n, ROWS, HALF), dtype)

    return pl.pallas_call(
        attend_kernel,
        out_shape=(
            jax.ShapeDtypeStruct((2 * ROWS, HALF), BF16),
            out(3, F32),
            out(3, BF16),
            out(2, BF16),
            out(2, BF16),
        ),
        grid_spec=pltpu.PrefetchScalarGridSpec(
            num_scalar_prefetch=1,
            grid=(HALF_HEADS,),
            in_specs=[raw] * 6 + [stack(4), stack(2), stack(4), stack(4), two],
            out_specs=(two, stack(3), stack(3), stack(2), stack(2)),
            scratch_shapes=[
                pltpu.VMEM((4 * ROWS, 2 * HEAD_DIM), BF16),
                pltpu.VMEM((4 * ROWS, HEAD_DIM), BF16),
                pltpu.VMEM((4 * ROWS, HEAD_DIM), BF16),
                pltpu.VMEM((2 * ROWS, 2 * HEAD_DIM), BF16),
                pltpu.VMEM((2 * ROWS, HEAD_DIM), BF16),
                pltpu.VMEM((2 * ROWS, 4 * ROWS), BF16),
                pltpu.VMEM((2 * ROWS, 4 * ROWS), BF16),
                pltpu.VMEM((2 * ROWS, HEAD_DIM), BF16),
                pltpu.VMEM((2 * ROWS, HEAD_DIM), F32),
                pltpu.VMEM((4 * ROWS, HEAD_DIM), F32),
                pltpu.VMEM((4 * ROWS, HEAD_DIM), F32),
            ],
        ),
        compiler_params=pltpu.CompilerParams(vmem_limit_bytes=VMEM_LIMIT),
        name="attend",
    )(core, *arrays, sib_kv, sib_q, far_own, far_sib, grad)


def tangent_kernel(tan, weight, own, sib):
    both = dot(tan[...], weight[...], NN)
    own[...] = both[:ROWS]
    sib[...] = both[ROWS:].astype(BF16)


def tangent(tan, weight):
    tile = 512
    return pl.pallas_call(
        tangent_kernel,
        grid=(WIDTH // tile,),
        out_shape=(
            jax.ShapeDtypeStruct((ROWS, WIDTH), F32),
            jax.ShapeDtypeStruct((ROWS, WIDTH), BF16),
        ),
        in_specs=[
            pl.BlockSpec((2 * ROWS, HALF), lambda i: (0, 0)),
            pl.BlockSpec((HALF, tile), lambda i: (0, i)),
        ],
        out_specs=(
            pl.BlockSpec((ROWS, tile), lambda i: (0, i)),
            pl.BlockSpec((ROWS, tile), lambda i: (0, i)),
        ),
        compiler_params=pltpu.CompilerParams(vmem_limit_bytes=VMEM_LIMIT),
        name="tangent",
    )(tan, weight)


def finish_first_kernel(core, own, sib, tan_own, tan_sib, q_out, tan_out):
    c = core[0]
    mine = pl.multiple_of(c * HALF, HALF)
    other = pl.multiple_of((1 - c) * HALF, HALF)
    tan_out[0] = (tan_own[...] + tan_sib[...].astype(F32)).astype(BF16)
    q_out[0, :, pl.ds(mine, HALF)] = own[0].astype(BF16)
    q_out[0, :, pl.ds(other, HALF)] = sib[0]


def finish_last_kernel(core, own, sib, near, cross, k_out, v_out):
    c = core[0]
    mine = pl.multiple_of(c * HALF, HALF)
    other = pl.multiple_of((1 - c) * HALF, HALF)
    for entry, ref in enumerate((k_out, v_out)):
        ref[0, :, pl.ds(mine, HALF)] = (own[entry + 1] + near[entry].astype(F32)).astype(BF16)
        ref[0, :, pl.ds(other, HALF)] = (
            sib[entry + 1].astype(F32) + cross[entry].astype(F32)
        ).astype(BF16)


def finish(kernel, name, core, *arrays):
    whole = pl.BlockSpec(memory_space=pltpu.VMEM)
    out = jax.ShapeDtypeStruct((1, ROWS, WIDTH), BF16)
    return pl.pallas_call(
        kernel,
        out_shape=(out, out),
        in_specs=[pl.BlockSpec(memory_space=pltpu.SMEM)] + [whole] * len(arrays),
        out_specs=(whole, whole),
        compiler_params=pltpu.CompilerParams(vmem_limit_bytes=VMEM_LIMIT),
        name=name,
    )(core, *arrays)


def body(q, k, v, tq, tk, tv, cot, out_weight):
    core = lax.axis_index("c").astype(jnp.int32).reshape(1)
    arrays = (q, tq, k, tk, v, tv)

    shard = permute(out_weight, swap_low_and_core)
    weight = lax.all_gather(shard, "z", axis=0, tiled=True)

    own_kv, sib_kv, sib_q = pack(core, arrays + (cot,))
    far_own = permute(own_kv, to_chip(1))
    sib_kv = permute(sib_kv, to_sibling)
    sib_q = permute(sib_q, to_sibling)
    far_sib = permute(sib_kv, to_chip(1))

    grad = project(cot, sib_q, weight)
    tan, own, sib, back_own, back_sib = attend(
        core, arrays, sib_kv, sib_q, far_own, far_sib, grad
    )
    back_own = permute(back_own, to_chip(-1))
    back_sib = permute(back_sib, to_chip(-1, cross=True))
    sib = permute(sib, to_sibling)
    tan_own, tan_sib = tangent(tan, weight)
    tan_sib = permute(tan_sib, to_sibling)
    query_grad, tangent_out = finish(
        finish_first_kernel, "finish_first", core, own, sib, tan_own, tan_sib
    )
    key_grad, value_grad = finish(
        finish_last_kernel, "finish_last", core, own, sib, back_own, back_sib
    )
    return tangent_out, query_grad, key_grad, value_grad


def solution(mesh):
    cut = Mesh(mesh.devices.reshape(SIZES), AXES)
    rows = P(("yl", "z"), ("x", "yh", "c"), None)
    return jax.shard_map(
        body,
        mesh=cut,
        in_specs=(rows,) * 7 + (P(("yl", "z"), None),),
        out_specs=(rows,) * 4,
        check_vma=False,
    )
```

time: 342 us -> 271 us (0.79)
  Pallas kernels: 0 us -> 152 us
  waiting for transfers between devices: 203 us -> 86.5 us
  local copies, waits for them, and re-layouts: 47.1 us -> 1.78 us
  matrix products: 43.2 us -> 0 us
  starting transfers between devices: 28.7 us -> 16.4 us
  other arithmetic: 5.18 us -> 0 us
    pallas_call x0 -> x6, Pallas kernels: none -> 152 us  [the longest x1 120 us: pack(): pl.pallas_call(pack_kernel, out_shape=(four, four, four), in_specs=[pl.Bl...]
    ppermute x12 -> x9, waiting for transfers between devices: 202 us -> 68.6 us  [permute(): return lax.ppermute(block, AXES, route)]
    dot_general x11 -> x0, matrix products: 40 us -> none  [the longest x1 8.98 us: body(): jnp.einsum('io,ao->ia', grad_out, full_weight, preferred_element_type=jnp...]
    all_gather x1, waiting for transfers between devices: 0.01 us -> 17.9 us  [body(): weight = lax.all_gather(shard, 'z', axis=0, tiled=True)]
    slice x8 -> x0, local copies, waits for them, and re-layouts: 16.4 us -> none  [the longest x2 6.92 us: body(): value_terms[rows:2 * rows]]
    ppermute x12 -> x9, starting transfers between devices: 28.7 us -> 16.4 us  [permute(): return lax.ppermute(block, AXES, route)]
    unnamed x45 -> x22, local copies, waits for them, and re-layouts: 12.6 us -> 1.78 us
    concatenate x6 -> x0, local copies, waits for them, and re-layouts: 9.04 us -> none  [the longest x3 5.89 us: body(): tk_window = jnp.concatenate([far_blocks[2], near_blocks[2], tk_own], axis=0)]
  transfers between devices with their start and end apart: 13 -> 10, of which waited for: 8 -> 7; matrix products, arithmetic and copies ran while one was open for 20% -> 0% of each run, Pallas kernels for 0% -> 49%
where the time goes in v1:
time: 271 us
  Pallas kernels  152 us (56%)
  waiting for transfers between devices  86.5 us (32%)
  starting transfers between devices  16.4 us (6%)
  between operations  14.2 us (5%)
    pallas_call x1, Pallas kernels, pack(): pl.pallas_call(pack_kernel, out_shape=(four, four, four), in_specs=[pl.Bl...  120 us
    ppermute x9, waiting for transfers between devices, permute(): return lax.ppermute(block, AXES, route)  68.6 us
    all_gather x1, waiting for transfers between devices, body(): weight = lax.all_gather(shard, 'z', axis=0, tiled=True)  17.9 us
    pallas_call x1, Pallas kernels, attend(): pl.pallas_call(attend_kernel, out_shape=(jax.ShapeDtypeStruct((2 * ROWS,...  17.7 us
    ppermute x9, starting transfers between devices, permute(): return lax.ppermute(block, AXES, route)  16.4 us
    pallas_call x1, Pallas kernels, project(): pl.pallas_call(project_kernel, grid=(HALF // tile,), out_shape=jax.ShapeD...  5.87 us
    pallas_call x1, Pallas kernels, tangent(): pl.pallas_call(tangent_kernel, grid=(WIDTH // tile,), out_shape=(jax.Shap...  5.7 us
  transfers between devices with their start and end apart: 10, of which 7 were waited for; matrix products, arithmetic and copies ran while one was open for 0% of the time, Pallas kernels for 49%

profile of v1, /device:TPU:1, one launch (start us, length us, event | category | flops | bytes accessed | tf_op | source)
XLA Modules:
  0.0 270.9 jit_solution(17321866440085272144)
XLA Ops:
  7.2 0.0 all-gather.2.cloned.1.call-start
  7.2 4.6 %collective-permute-start.4 = (bf16[160,2560]{1,0:T(8,128)(2,1)}, bf16[160,2560]{1,0:T(8,128)(2,1)S(1)}, u32[]{:S(2)}, u32[]{:S(2)}) collective-permute-start(bf16[160,2560]{1,0:T(8,128)(2,1)} %param.15), channel_id=1, source_target_pairs={{0,0},{1,128},{2,2},{3,130},{4,4},{5,132},{6,6},{7,134},{8,8},{9,1... | collective-permute-start | bytes 2457608 | tf_op jit(solution)/shard_map/ppermute | solution.py:38
  11.8 10.2 %collective-permute-done.4 = bf16[160,2560]{1,0:T(8,128)(2,1)S(1)} collective-permute-done((bf16[160,2560]{1,0:T(8,128)(2,1)}, bf16[160,2560]{1,0:T(8,128)(2,1)S(1)}, u32[]{:S(2)}, u32[]{:S(2)}) %collective-permute-start.4) | collective-permute-done | bytes 819232 | tf_op jit(solution)/shard_map/ppermute | solution.py:38
  22.0 0.0 copy-start.10
  22.0 0.9 copy-done.10
  23.0 0.0 all-gather.2.cloned.1.call-update
  23.0 0.0 copy-start.3
  23.0 120.3 %pack.1 = (bf16[4,128,1280]{2,1,0:T(8,128)(2,1)}, bf16[4,128,1280]{2,1,0:T(8,128)(2,1)}, bf16[4,128,1280]{2,1,0:T(8,128)(2,1)}) custom-call(s32[1]{0:T(128)} %bitcast.core, bf16[1,128,2560]{2,1,0:T(8,128)(2,1)} %q.3, bf16[1,128,2560]{2,1,0:T(8,128)(2,1)} %tq.3, bf16[1,128,2560]{2,1,0:T(8,128)(2,1)} %k.3, bf16[1,128,2560]{2,1,0:T(8,128)(2,1)} %tk.3, ...), custom_call_target="tpu_custom_call" | custom-call | tf_op jit(solution)/shard_map/pack/pallas_call | solution.py:85
  143.3 0.1 collective-permute-start
  143.4 0.5 collective-permute-start.1
  143.9 0.0 copy-start.4
  143.9 0.0 copy-start.5
  143.9 2.8 %collective-permute-start.2 = (bf16[4,128,1280]{2,1,0:T(8,128)(2,1)}, bf16[4,128,1280]{2,1,0:T(8,128)(2,1)}, u32[]{:S(2)}, u32[]{:S(2)}) collective-permute-start(bf16[4,128,1280]{2,1,0:T(8,128)(2,1)} %get-tuple-element.20), channel_id=1, source_target_pairs={{0,2},{1,3},{2,4},{3,5},{4,6},{5,7},{6,8},{7,9},{8,10},{9,11},{10,... | collective-permute-start | bytes 3932168 | tf_op jit(solution)/shard_map/ppermute | solution.py:38
  146.7 0.9 collective-permute-done.sib_kv
  147.7 2.8 %collective-permute-start.3 = (bf16[4,128,1280]{2,1,0:T(8,128)(2,1)}, bf16[4,128,1280]{2,1,0:T(8,128)(2,1)}, u32[]{:S(2)}, u32[]{:S(2)}) collective-permute-start(bf16[4,128,1280]{2,1,0:T(8,128)(2,1)} %collective-permute-done.sib_kv), channel_id=1, source_target_pairs={{0,2},{1,3},{2,4},{3,5},{4,6},{5,7},{6,8},{7,9},{8,10},{9,11},{10,... | collective-permute-start | bytes 3932168 | tf_op jit(solution)/shard_map/ppermute | solution.py:38
  150.4 0.0 collective-permute-done.1.sib_q
  150.4 0.0 copy-start.1
  150.4 17.9 %all-gather.2.cloned.1.call-done.weight = bf16[1280,2560]{1,0:T(8,128)(2,1)} async-done(((bf16[160,2560]{1,0:T(8,128)(2,1)}), bf16[1280,2560]{1,0:T(8,128)(2,1)}) %all-gather.2.cloned.1.call-update) | async-done | bytes 6553616 | tf_op jit(solution)/shard_map/all_gather | solution.py:321
  168.3 0.0 copy-done.3
  168.3 0.0 copy-start.6
  168.3 0.0 copy-start.7
  168.3 0.0 copy-start.8
  168.4 0.0 copy-start.9
  168.4 5.9 %project.1.grad = bf16[256,1280]{1,0:T(8,128)(2,1)S(1)} custom-call(bf16[1,128,2560]{2,1,0:T(8,128)(2,1)S(1)} %copy-done.3, bf16[4,128,1280]{2,1,0:T(8,128)(2,1)S(1)} %collective-permute-done.1.sib_q, bf16[1280,2560]{1,0:T(8,128)(2,1)} %all-gather.2.cloned.1.call-done.weight), custom_call_target="tpu_custom_call" | custom-call | tf_op jit(solution)/shard_map/project/pallas_call | solution.py:109
  174.2 0.0 copy-done.1
  174.3 0.0 copy-start.2
  174.3 0.8 copy-done.2
  175.1 3.1 %collective-permute-done.2.far_own = bf16[4,128,1280]{2,1,0:T(8,128)(2,1)} collective-permute-done((bf16[4,128,1280]{2,1,0:T(8,128)(2,1)}, bf16[4,128,1280]{2,1,0:T(8,128)(2,1)}, u32[]{:S(2)}, u32[]{:S(2)}) %collective-permute-start.2) | collective-permute-done | bytes 1310752 | tf_op jit(solution)/shard_map/ppermute | solution.py:38
  178.2 28.1 %collective-permute-done.3.far_sib = bf16[4,128,1280]{2,1,0:T(8,128)(2,1)} collective-permute-done((bf16[4,128,1280]{2,1,0:T(8,128)(2,1)}, bf16[4,128,1280]{2,1,0:T(8,128)(2,1)}, u32[]{:S(2)}, u32[]{:S(2)}) %collective-permute-start.3) | collective-permute-done | bytes 1310752 | tf_op jit(solution)/shard_map/ppermute | solution.py:38
  206.3 0.0 copy-done.4
  206.3 0.0 copy-done.5
  206.3 0.0 copy-done.6
  206.3 0.0 copy-done.7
  206.3 0.0 copy-done.8
  206.3 0.0 copy-done.9
  206.3 17.7 %attend.1 = (bf16[256,1280]{1,0:T(8,128)(2,1)S(1)}, f32[3,128,1280]{2,1,0:T(8,128)}, bf16[3,128,1280]{2,1,0:T(8,128)(2,1)}, bf16[2,128,1280]{2,1,0:T(8,128)(2,1)S(1)}, bf16[2,128,1280]{2,1,0:T(8,128)(2,1)S(1)}) custom-call(s32[1]{0:T(128)} %bitcast.core, bf16[1,128,2560]{2,1,0:T(8,128)(2,1)S(1)} %copy-done.4, bf16[1,128,2560]{2,1,0:T(8,128)(2,1)S(1)} %copy-done.5, ...), custom_call_target="tpu_custom_call" | custom-call | tf_op jit(solution)/shard_map/attend/pallas_call | solution.py:222
  224.0 0.9 collective-permute-start.5
  224.9 0.0 copy-start
  224.9 5.7 %tangent.1 = (f32[128,2560]{1,0:T(8,128)S(1)}, bf16[128,2560]{1,0:T(8,128)(2,1)S(1)}) custom-call(bf16[256,1280]{1,0:T(8,128)(2,1)S(1)} %get-tuple-element.23.tan, bf16[1280,2560]{1,0:T(8,128)(2,1)} %all-gather.2.cloned.1.call-done.weight), custom_call_target="tpu_custom_call" | custom-call | tf_op jit(solution)/shard_map/tangent/pallas_call | solution.py:263
  230.6 0.1 collective-permute-start.6
  230.7 3.0 %collective-permute-start.7 = (bf16[2,128,1280]{2,1,0:T(8,128)(2,1)S(1)}, bf16[2,128,1280]{2,1,0:T(8,128)(2,1)S(1)}, u32[]{:S(2)}, u32[]{:S(2)}) collective-permute-start(bf16[2,128,1280]{2,1,0:T(8,128)(2,1)S(1)} %get-tuple-element.28), channel_id=1, source_target_pairs={{0,14},{1,15},{2,0},{3,1},{4,2},{5,3},{6,4},{7,5},{8,6},{9,7},{10,... | collective-permute-start | bytes 1966088 | tf_op jit(solution)/shard_map/ppermute | solution.py:38
  233.6 1.7 collective-permute-start.8
  235.3 0.0 collective-permute-done.6.tan_sib
  235.3 0.0 collective-permute-done.5.sib
  235.3 0.0 copy-done
  235.3 1.2 finish_first.1
  236.5 11.6 %collective-permute-done.7.near = bf16[2,128,1280]{2,1,0:T(8,128)(2,1)S(1)} collective-permute-done((bf16[2,128,1280]{2,1,0:T(8,128)(2,1)S(1)}, bf16[2,128,1280]{2,1,0:T(8,128)(2,1)S(1)}, u32[]{:S(2)}, u32[]{:S(2)}) %collective-permute-start.7) | collective-permute-done | bytes 655392 | tf_op jit(solution)/shard_map/ppermute | solution.py:38
  248.2 14.6 %collective-permute-done.8.cross = bf16[2,128,1280]{2,1,0:T(8,128)(2,1)S(1)} collective-permute-done((bf16[2,128,1280]{2,1,0:T(8,128)(2,1)S(1)}, bf16[2,128,1280]{2,1,0:T(8,128)(2,1)S(1)}, u32[]{:S(2)}, u32[]{:S(2)}) %collective-permute-start.8) | collective-permute-done | bytes 655392 | tf_op jit(solution)/shard_map/ppermute | solution.py:38
  262.8 1.2 finish_last.1
Async XLA Ops:
  7.2 161.2 %all-gather.2.cloned.1.call-start = ((), (), s32[]{:S(2)}) async-start(), calls=%async_computation | async-start | bytes 7372800 | tf_op jit(solution)/shard_map/all_gather | solution.py:321
  7.2 14.8 %collective-permute-start.4 = (bf16[160,2560]{1,0:T(8,128)(2,1)}, bf16[160,2560]{1,0:T(8,128)(2,1)S(1)}, u32[]{:S(2)}, u32[]{:S(2)}) collective-permute-start(bf16[160,2560]{1,0:T(8,128)(2,1)} %param.15), channel_id=1, source_target_pairs={{0,0},{1,128},{2,2},{3,130},{4,4},{5,132},{6,6},{7,134},{8,8},{9,1... | collective-permute-start | bytes 2457608 | tf_op jit(solution)/shard_map/ppermute | solution.py:38
  22.0 0.9 copy-start.10
  23.0 145.4 %copy-start.3 = (bf16[1,128,2560]{2,1,0:T(8,128)(2,1)S(1)}, bf16[1,128,2560]{2,1,0:T(8,128)(2,1)}, u32[]{:S(2)}) copy-start(bf16[1,128,2560]{2,1,0:T(8,128)(2,1)} %cot.3) | copy-start | bytes 1966084
  143.3 4.3 %collective-permute-start = (bf16[4,128,1280]{2,1,0:T(8,128)(2,1)}, bf16[4,128,1280]{2,1,0:T(8,128)(2,1)}, u32[]{:S(2)}, u32[]{:S(2)}) collective-permute-start(bf16[4,128,1280]{2,1,0:T(8,128)(2,1)} %get-tuple-element.18), channel_id=1, source_target_pairs={{0,1},{1,0},{2,3},{3,2},{4,5},{5,4},{6,7},{7,6},{8,9},{9,8},{10,11... | collective-permute-start | bytes 3932168 | tf_op jit(solution)/shard_map/ppermute | solution.py:38
  143.4 7.0 %collective-permute-start.1 = (bf16[4,128,1280]{2,1,0:T(8,128)(2,1)}, bf16[4,128,1280]{2,1,0:T(8,128)(2,1)S(1)}, u32[]{:S(2)}, u32[]{:S(2)}) collective-permute-start(bf16[4,128,1280]{2,1,0:T(8,128)(2,1)} %get-tuple-element.19), channel_id=1, source_target_pairs={{0,1},{1,0},{2,3},{3,2},{4,5},{5,4},{6,7},{7,6},{8,9},{9,8},{10,11... | collective-permute-start | bytes 3932168 | tf_op jit(solution)/shard_map/ppermute | solution.py:38
  143.9 62.4 %copy-start.4 = (bf16[1,128,2560]{2,1,0:T(8,128)(2,1)S(1)}, bf16[1,128,2560]{2,1,0:T(8,128)(2,1)}, u32[]{:S(2)}) copy-start(bf16[1,128,2560]{2,1,0:T(8,128)(2,1)} %q.3) | copy-start | bytes 1966084
  143.9 62.4 %copy-start.5 = (bf16[1,128,2560]{2,1,0:T(8,128)(2,1)S(1)}, bf16[1,128,2560]{2,1,0:T(8,128)(2,1)}, u32[]{:S(2)}) copy-start(bf16[1,128,2560]{2,1,0:T(8,128)(2,1)} %tq.3) | copy-start | bytes 1966084
  143.9 34.3 %collective-permute-start.2 = (bf16[4,128,1280]{2,1,0:T(8,128)(2,1)}, bf16[4,128,1280]{2,1,0:T(8,128)(2,1)}, u32[]{:S(2)}, u32[]{:S(2)}) collective-permute-start(bf16[4,128,1280]{2,1,0:T(8,128)(2,1)} %get-tuple-element.20), channel_id=1, source_target_pairs={{0,2},{1,3},{2,4},{3,5},{4,6},{5,7},{6,8},{7,9},{8,10},{9,11},{10,... | collective-permute-start | bytes 3932168 | tf_op jit(solution)/shard_map/ppermute | solution.py:38
  147.7 58.6 %collective-permute-start.3 = (bf16[4,128,1280]{2,1,0:T(8,128)(2,1)}, bf16[4,128,1280]{2,1,0:T(8,128)(2,1)}, u32[]{:S(2)}, u32[]{:S(2)}) collective-permute-start(bf16[4,128,1280]{2,1,0:T(8,128)(2,1)} %collective-permute-done.sib_kv), channel_id=1, source_target_pairs={{0,2},{1,3},{2,4},{3,5},{4,6},{5,7},{6,8},{7,9},{8,10},{9,11},{10,... | collective-permute-start | bytes 3932168 | tf_op jit(solution)/shard_map/ppermute | solution.py:38
  150.4 23.8 %copy-start.1 = (bf16[4,128,1280]{2,1,0:T(8,128)(2,1)}, bf16[4,128,1280]{2,1,0:T(8,128)(2,1)S(1)}, u32[]{:S(2)}) copy-start(bf16[4,128,1280]{2,1,0:T(8,128)(2,1)S(1)} %collective-permute-done.1.sib_q) | copy-start | bytes 3932164
  168.3 38.0 %copy-start.6 = (bf16[1,128,2560]{2,1,0:T(8,128)(2,1)S(1)}, bf16[1,128,2560]{2,1,0:T(8,128)(2,1)}, u32[]{:S(2)}) copy-start(bf16[1,128,2560]{2,1,0:T(8,128)(2,1)} %k.3) | copy-start | bytes 1966084
  168.3 38.0 %copy-start.7 = (bf16[1,128,2560]{2,1,0:T(8,128)(2,1)S(1)}, bf16[1,128,2560]{2,1,0:T(8,128)(2,1)}, u32[]{:S(2)}) copy-start(bf16[1,128,2560]{2,1,0:T(8,128)(2,1)} %tk.3) | copy-start | bytes 1966084
  168.3 38.0 %copy-start.8 = (bf16[1,128,2560]{2,1,0:T(8,128)(2,1)S(1)}, bf16[1,128,2560]{2,1,0:T(8,128)(2,1)}, u32[]{:S(2)}) copy-start(bf16[1,128,2560]{2,1,0:T(8,128)(2,1)} %v.3) | copy-start | bytes 1966084
  168.4 38.0 %copy-start.9 = (bf16[1,128,2560]{2,1,0:T(8,128)(2,1)S(1)}, bf16[1,128,2560]{2,1,0:T(8,128)(2,1)}, u32[]{:S(2)}) copy-start(bf16[1,128,2560]{2,1,0:T(8,128)(2,1)} %tv.3) | copy-start | bytes 1966084
  174.3 0.8 copy-start.2
  224.0 11.3 %collective-permute-start.5 = (bf16[3,128,1280]{2,1,0:T(8,128)(2,1)}, bf16[3,128,1280]{2,1,0:T(8,128)(2,1)S(1)}, u32[]{:S(2)}, u32[]{:S(2)}) collective-permute-start(bf16[3,128,1280]{2,1,0:T(8,128)(2,1)} %get-tuple-element.22), channel_id=1, source_target_pairs={{0,1},{1,0},{2,3},{3,2},{4,5},{5,4},{6,7},{7,6},{8,9},{9,8},{10,11... | collective-permute-start | bytes 2949128 | tf_op jit(solution)/shard_map/ppermute | solution.py:38
  224.9 10.4 %copy-start = (f32[3,128,1280]{2,1,0:T(8,128)S(1)}, f32[3,128,1280]{2,1,0:T(8,128)}, u32[]{:S(2)}) copy-start(f32[3,128,1280]{2,1,0:T(8,128)} %get-tuple-element.21.own) | copy-start | bytes 5898244
  230.6 4.7 %collective-permute-start.6 = (bf16[128,2560]{1,0:T(8,128)(2,1)S(1)}, bf16[128,2560]{1,0:T(8,128)(2,1)S(1)}, u32[]{:S(2)}, u32[]{:S(2)}) collective-permute-start(bf16[128,2560]{1,0:T(8,128)(2,1)S(1)} %get-tuple-element.25), channel_id=1, source_target_pairs={{0,1},{1,0},{2,3},{3,2},{4,5},{5,4},{6,7},{7,6},{8,9},{9,8},{10,11... | collective-permute-start | bytes 1966088 | tf_op jit(solution)/shard_map/ppermute | solution.py:38
  230.7 17.5 %collective-permute-start.7 = (bf16[2,128,1280]{2,1,0:T(8,128)(2,1)S(1)}, bf16[2,128,1280]{2,1,0:T(8,128)(2,1)S(1)}, u32[]{:S(2)}, u32[]{:S(2)}) collective-permute-start(bf16[2,128,1280]{2,1,0:T(8,128)(2,1)S(1)} %get-tuple-element.28), channel_id=1, source_target_pairs={{0,14},{1,15},{2,0},{3,1},{4,2},{5,3},{6,4},{7,5},{8,6},{9,7},{10,... | collective-permute-start | bytes 1966088 | tf_op jit(solution)/shard_map/ppermute | solution.py:38
  233.6 29.1 %collective-permute-start.8 = (bf16[2,128,1280]{2,1,0:T(8,128)(2,1)S(1)}, bf16[2,128,1280]{2,1,0:T(8,128)(2,1)S(1)}, u32[]{:S(2)}, u32[]{:S(2)}) collective-permute-start(bf16[2,128,1280]{2,1,0:T(8,128)(2,1)S(1)} %get-tuple-element.29), channel_id=1, source_target_pairs={{0,15},{1,14},{2,1},{3,0},{4,3},{5,2},{6,5},{7,4},{8,7},{9,6},{10,... | collective-permute-start | bytes 1966088 | tf_op jit(solution)/shard_map/ppermute | solution.py:38
Sparse Core Ops, SparseCore 0:
  23.1 145.1 all-gather.1

commit v2 on v1

--- a/solution.py
+++ b/solution.py
@@ -54,40 +54,31 @@
     return c, z, x, yh, yl
 
 
-def pack_kernel(core, q, tq, k, tk, v, tv, cot, own_kv, sib_kv, sib_q, sems):
+def pack_kernel(core, q, tq, k, tk, v, tv, cot, own_kv, sib_kv, sib_q):
     c = core[0]
-    mine = pl.multiple_of(c * HALF, HALF)
-    other = pl.multiple_of((1 - c) * HALF, HALF)
-    copies = []
-
-    def put(source, start, target, entry):
-        copy = pltpu.make_async_copy(
-            source.at[0, :, pl.ds(start, HALF)], target.at[entry], sems.at[len(copies)]
-        )
-        copy.start()
-        copies.append(copy)
-
+    mine = pl.ds(pl.multiple_of(c * HALF, HALF), HALF)
+    other = pl.ds(pl.multiple_of((1 - c) * HALF, HALF), HALF)
     for entry, source in enumerate((k, tk, v, tv)):
-        put(source, mine, own_kv, entry)
-    for entry, source in enumerate((k, tk, v, tv)):
-        put(source, other, sib_kv, entry)
+        own_kv[entry] = source[0, :, mine]
+        sib_kv[entry] = source[0, :, other]
     for entry, source in enumerate((q, tq)):
-        put(source, other, sib_q, entry)
-    put(cot, 0, sib_q, 2)
-    put(cot, HALF, sib_q, 3)
-    for copy in copies:
-        copy.wait()
+        sib_q[entry] = source[0, :, other]
+    sib_q[2] = cot[0, :, :HALF]
+    sib_q[3] = cot[0, :, HALF:]
 
 
 def pack(core, arrays):
-    anywhere = pl.BlockSpec(memory_space=pl.ANY)
+    tile = 32
+    raw = pl.BlockSpec((1, tile, WIDTH), lambda i: (0, i, 0))
     four = jax.ShapeDtypeStruct((4, ROWS, HALF), BF16)
+    out = pl.BlockSpec((4, tile, HALF), lambda i: (0, i, 0))
     return pl.pallas_call(
         pack_kernel,
+        grid=(ROWS // tile,),
         out_shape=(four, four, four),
-        in_specs=[pl.BlockSpec(memory_space=pltpu.SMEM)] + [anywhere] * 7,
-        out_specs=(anywhere, anywhere, anywhere),
-        scratch_shapes=[pltpu.SemaphoreType.DMA((12,))],
+        in_specs=[pl.BlockSpec(memory_space=pltpu.SMEM)] + [raw] * 7,
+        out_specs=(out, out, out),
+        compiler_params=pltpu.CompilerParams(vmem_limit_bytes=VMEM_LIMIT),
         name="pack",
     )(core, *arrays)
 

time: 271 us -> 176 us (0.65)
  Pallas kernels: 152 us -> 34.2 us
  waiting for transfers between devices: 86.5 us -> 99.5 us
  local copies, waits for them, and re-layouts: 1.78 us -> 9.37 us
    pallas_call x1, Pallas kernels: 120 us -> 2.46 us  [pack(): pl.pallas_call(pack_kernel, grid=(ROWS // tile,), out_shape=(four, four,...]
    all_gather x1, waiting for transfers between devices: 17.9 us -> 61.7 us  [body(): weight = lax.all_gather(shard, 'z', axis=0, tiled=True)]
    ppermute x9, waiting for transfers between devices: 68.6 us -> 37.8 us  [permute(): return lax.ppermute(block, AXES, route)]
    unnamed x22 -> x36, local copies, waits for them, and re-layouts: 1.78 us -> 9.37 us
  transfers between devices with their start and end apart: 10 -> 10, of which waited for: 7 -> 5; matrix products, arithmetic and copies ran while one was open for 0% -> 0% of each run, Pallas kernels for 49% -> 9%
where the time goes in v2:
time: 176 us; the launch traced here: 174 us
  waiting for transfers between devices  99.5 us (57%)
  Pallas kernels  34.2 us (19%)
  starting transfers between devices  17.3 us (10%)
  between operations  14.2 us (8%)
  local copies, waits for them, and re-layouts  9.37 us (5%)
    all_gather x1, waiting for transfers between devices, body(): weight = lax.all_gather(shard, 'z', axis=0, tiled=True)  61.7 us
    ppermute x9, waiting for transfers between devices, permute(): return lax.ppermute(block, AXES, route)  37.8 us
    pallas_call x1, Pallas kernels, attend(): pl.pallas_call(attend_kernel, out_shape=(jax.ShapeDtypeStruct((2 * ROWS,...  17.7 us
    ppermute x9, starting transfers between devices, permute(): return lax.ppermute(block, AXES, route)  17.2 us
    unnamed x36, local copies, waits for them, and re-layouts  9.37 us
    pallas_call x1, Pallas kernels, project(): pl.pallas_call(project_kernel, grid=(HALF // tile,), out_shape=jax.ShapeD...  5.88 us
    pallas_call x1, Pallas kernels, tangent(): pl.pallas_call(tangent_kernel, grid=(WIDTH // tile,), out_shape=(jax.Shap...  5.7 us
  transfers between devices with their start and end apart: 10, of which 5 were waited for; matrix products, arithmetic and copies ran while one was open for 0% of the time, Pallas kernels for 9%

profile of v2, /device:TPU:1, one launch (start us, length us, event | category | flops | bytes accessed | tf_op | source)
XLA Modules:
  0.0 174.5 jit_solution(16506637993506389288)
XLA Ops:
  7.2 0.0 all-gather.2.cloned.1.call-start
  7.2 4.6 %collective-permute-start.4 = (bf16[160,2560]{1,0:T(8,128)(2,1)}, bf16[160,2560]{1,0:T(8,128)(2,1)S(1)}, u32[]{:S(2)}, u32[]{:S(2)}) collective-permute-start(bf16[160,2560]{1,0:T(8,128)(2,1)} %param.15), channel_id=1, source_target_pairs={{0,0},{1,128},{2,2},{3,130},{4,4},{5,132},{6,6},{7,134},{8,8},{9,1... | collective-permute-start | bytes 2457608 | tf_op jit(solution)/shard_map/ppermute | solution.py:38
  11.8 10.2 %collective-permute-done.4 = bf16[160,2560]{1,0:T(8,128)(2,1)S(1)} collective-permute-done((bf16[160,2560]{1,0:T(8,128)(2,1)}, bf16[160,2560]{1,0:T(8,128)(2,1)S(1)}, u32[]{:S(2)}, u32[]{:S(2)}) %collective-permute-start.4) | collective-permute-done | bytes 819232 | tf_op jit(solution)/shard_map/ppermute | solution.py:38
  22.0 0.0 copy-start.17
  22.0 0.9 copy-done.17
  22.9 0.0 all-gather.2.cloned.1.call-update
  23.0 0.0 copy-start.3
  23.0 1.1 copy-done.3
  24.1 0.0 copy-start.5
  24.1 1.1 copy-done.5
  25.1 0.0 copy-start.7
  25.1 1.1 copy-done.7
  26.2 0.0 copy-start.9
  26.2 1.1 copy-done.9
  27.3 0.0 copy-start.11
  27.3 1.1 copy-done.11
  28.4 0.0 copy-start.13
  28.4 1.1 copy-done.13
  29.5 0.0 copy-start.15
  29.5 1.1 copy-done.15
  30.6 0.0 copy-start.4
  30.6 2.5 %pack.1 = (bf16[4,128,1280]{2,1,0:T(8,128)(2,1)}, bf16[4,128,1280]{2,1,0:T(8,128)(2,1)}, bf16[4,128,1280]{2,1,0:T(8,128)(2,1)}) custom-call(s32[1]{0:T(128)} %bitcast.core, bf16[1,128,2560]{2,1,0:T(8,128)(2,1)S(1)} %copy-done.5, bf16[1,128,2560]{2,1,0:T(8,128)(2,1)S(1)} %copy-done.7, bf16[1,128,2560]{2,1,0:T(8,128)(2,1)S(1)} %copy-done.9, ...), custom_call_target="tpu_custom_call" | custom-call | tf_op jit(solution)/shard_map/pack/pallas_call | solution.py:75
  33.0 0.0 collective-permute-start
  33.0 0.5 collective-permute-start.1
  33.6 0.0 copy-start.6
  33.6 0.0 copy-start.8
  33.6 2.8 %collective-permute-start.2 = (bf16[4,128,1280]{2,1,0:T(8,128)(2,1)}, bf16[4,128,1280]{2,1,0:T(8,128)(2,1)}, u32[]{:S(2)}, u32[]{:S(2)}) collective-permute-start(bf16[4,128,1280]{2,1,0:T(8,128)(2,1)} %get-tuple-element.20), channel_id=1, source_target_pairs={{0,2},{1,3},{2,4},{3,5},{4,6},{5,7},{6,8},{7,9},{8,10},{9,11},{10,... | collective-permute-start | bytes 3932168 | tf_op jit(solution)/shard_map/ppermute | solution.py:38
  36.3 1.9 %collective-permute-done.sib_kv = bf16[4,128,1280]{2,1,0:T(8,128)(2,1)} collective-permute-done((bf16[4,128,1280]{2,1,0:T(8,128)(2,1)}, bf16[4,128,1280]{2,1,0:T(8,128)(2,1)}, u32[]{:S(2)}, u32[]{:S(2)}) %collective-permute-start) | collective-permute-done | bytes 1310752 | tf_op jit(solution)/shard_map/ppermute | solution.py:38
  38.3 2.8 %collective-permute-start.3 = (bf16[4,128,1280]{2,1,0:T(8,128)(2,1)}, bf16[4,128,1280]{2,1,0:T(8,128)(2,1)}, u32[]{:S(2)}, u32[]{:S(2)}) collective-permute-start(bf16[4,128,1280]{2,1,0:T(8,128)(2,1)} %collective-permute-done.sib_kv), channel_id=1, source_target_pairs={{0,2},{1,3},{2,4},{3,5},{4,6},{5,7},{6,8},{7,9},{8,10},{9,11},{10,... | collective-permute-start | bytes 3932168 | tf_op jit(solution)/shard_map/ppermute | solution.py:38
  41.1 0.0 collective-permute-done.1.sib_q
  41.1 0.0 copy-start.1
  41.1 61.7 %all-gather.2.cloned.1.call-done.weight = bf16[1280,2560]{1,0:T(8,128)(2,1)} async-done(((bf16[160,2560]{1,0:T(8,128)(2,1)}), bf16[1280,2560]{1,0:T(8,128)(2,1)}) %all-gather.2.cloned.1.call-update) | async-done | bytes 6553616 | tf_op jit(solution)/shard_map/all_gather | solution.py:312
  102.7 0.0 copy-done.4
  102.7 0.0 copy-start.10
  102.7 0.0 copy-start.12
  102.7 0.0 copy-start.14
  102.7 0.0 copy-start.16
  102.7 5.9 %project.1.grad = bf16[256,1280]{1,0:T(8,128)(2,1)S(1)} custom-call(bf16[1,128,2560]{2,1,0:T(8,128)(2,1)S(1)} %copy-done.4, bf16[4,128,1280]{2,1,0:T(8,128)(2,1)S(1)} %collective-permute-done.1.sib_q, bf16[1280,2560]{1,0:T(8,128)(2,1)} %all-gather.2.cloned.1.call-done.weight), custom_call_target="tpu_custom_call" | custom-call | tf_op jit(solution)/shard_map/project/pallas_call | solution.py:100
  108.6 0.0 copy-done.1
  108.6 0.0 copy-start.2
  108.7 0.8 copy-done.2
  109.5 0.0 collective-permute-done.2.far_own
  109.5 0.0 collective-permute-done.3.far_sib
  109.5 0.0 copy-done.6
  109.5 0.0 copy-done.8
  109.5 0.0 copy-done.10
  109.5 0.0 copy-done.12
  109.5 0.0 copy-done.14
  109.5 0.0 copy-done.16
  109.5 17.7 %attend.1 = (bf16[256,1280]{1,0:T(8,128)(2,1)S(1)}, f32[3,128,1280]{2,1,0:T(8,128)}, bf16[3,128,1280]{2,1,0:T(8,128)(2,1)}, bf16[2,128,1280]{2,1,0:T(8,128)(2,1)S(1)}, bf16[2,128,1280]{2,1,0:T(8,128)(2,1)S(1)}) custom-call(s32[1]{0:T(128)} %bitcast.core, bf16[1,128,2560]{2,1,0:T(8,128)(2,1)S(1)} %copy-done.6, bf16[1,128,2560]{2,1,0:T(8,128)(2,1)S(1)} %copy-done.8, ...), custom_call_target="tpu_custom_call" | custom-call | tf_op jit(solution)/shard_map/attend/pallas_call | solution.py:213
  127.2 0.7 collective-permute-start.5
  127.9 0.0 copy-start
  127.9 5.7 %tangent.1 = (f32[128,2560]{1,0:T(8,128)S(1)}, bf16[128,2560]{1,0:T(8,128)(2,1)S(1)}) custom-call(bf16[256,1280]{1,0:T(8,128)(2,1)S(1)} %get-tuple-element.23.tan, bf16[1280,2560]{1,0:T(8,128)(2,1)} %all-gather.2.cloned.1.call-done.weight), custom_call_target="tpu_custom_call" | custom-call | tf_op jit(solution)/shard_map/tangent/pallas_call | solution.py:254
  133.6 0.1 collective-permute-start.6
  133.7 4.9 %collective-permute-start.7 = (bf16[2,128,1280]{2,1,0:T(8,128)(2,1)S(1)}, bf16[2,128,1280]{2,1,0:T(8,128)(2,1)S(1)}, u32[]{:S(2)}, u32[]{:S(2)}) collective-permute-start(bf16[2,128,1280]{2,1,0:T(8,128)(2,1)S(1)} %get-tuple-element.28), channel_id=1, source_target_pairs={{0,14},{1,15},{2,0},{3,1},{4,2},{5,3},{6,4},{7,5},{8,6},{9,7},{10,... | collective-permute-start | bytes 1966088 | tf_op jit(solution)/shard_map/ppermute | solution.py:38
  138.6 0.8 collective-permute-start.8
  139.5 0.0 collective-permute-done.6.tan_sib
  139.5 0.0 collective-permute-done.5.sib
  139.5 0.0 copy-done
  139.5 1.2 finish_first.1
  140.7 11.6 %collective-permute-done.7.near = bf16[2,128,1280]{2,1,0:T(8,128)(2,1)S(1)} collective-permute-done((bf16[2,128,1280]{2,1,0:T(8,128)(2,1)S(1)}, bf16[2,128,1280]{2,1,0:T(8,128)(2,1)S(1)}, u32[]{:S(2)}, u32[]{:S(2)}) %collective-permute-start.7) | collective-permute-done | bytes 655392 | tf_op jit(solution)/shard_map/ppermute | solution.py:38
  152.3 14.0 %collective-permute-done.8.cross = bf16[2,128,1280]{2,1,0:T(8,128)(2,1)S(1)} collective-permute-done((bf16[2,128,1280]{2,1,0:T(8,128)(2,1)S(1)}, bf16[2,128,1280]{2,1,0:T(8,128)(2,1)S(1)}, u32[]{:S(2)}, u32[]{:S(2)}) %collective-permute-start.8) | collective-permute-done | bytes 655392 | tf_op jit(solution)/shard_map/ppermute | solution.py:38
  166.4 1.3 finish_last.1
Async XLA Ops:
  7.2 95.6 %all-gather.2.cloned.1.call-start = ((), (), s32[]{:S(2)}) async-start(), calls=%async_computation | async-start | bytes 7372800 | tf_op jit(solution)/shard_map/all_gather | solution.py:312
  7.2 14.8 %collective-permute-start.4 = (bf16[160,2560]{1,0:T(8,128)(2,1)}, bf16[160,2560]{1,0:T(8,128)(2,1)S(1)}, u32[]{:S(2)}, u32[]{:S(2)}) collective-permute-start(bf16[160,2560]{1,0:T(8,128)(2,1)} %param.15), channel_id=1, source_target_pairs={{0,0},{1,128},{2,2},{3,130},{4,4},{5,132},{6,6},{7,134},{8,8},{9,1... | collective-permute-start | bytes 2457608 | tf_op jit(solution)/shard_map/ppermute | solution.py:38
  22.0 0.9 copy-start.17
  23.0 1.1 copy-start.3
  24.1 1.1 copy-start.5
  25.1 1.1 copy-start.7
  26.2 1.1 copy-start.9
  27.3 1.1 copy-start.11
  28.4 1.1 copy-start.13
  29.5 1.1 copy-start.15
  30.6 72.1 %copy-start.4 = (bf16[1,128,2560]{2,1,0:T(8,128)(2,1)S(1)}, bf16[1,128,2560]{2,1,0:T(8,128)(2,1)}, u32[]{:S(2)}) copy-start(bf16[1,128,2560]{2,1,0:T(8,128)(2,1)} %cot.3) | copy-start | bytes 1966084
  33.0 5.2 %collective-permute-start = (bf16[4,128,1280]{2,1,0:T(8,128)(2,1)}, bf16[4,128,1280]{2,1,0:T(8,128)(2,1)}, u32[]{:S(2)}, u32[]{:S(2)}) collective-permute-start(bf16[4,128,1280]{2,1,0:T(8,128)(2,1)} %get-tuple-element.18), channel_id=1, source_target_pairs={{0,1},{1,0},{2,3},{3,2},{4,5},{5,4},{6,7},{7,6},{8,9},{9,8},{10,11... | collective-permute-start | bytes 3932168 | tf_op jit(solution)/shard_map/ppermute | solution.py:38
  33.0 8.0 %collective-permute-start.1 = (bf16[4,128,1280]{2,1,0:T(8,128)(2,1)}, bf16[4,128,1280]{2,1,0:T(8,128)(2,1)S(1)}, u32[]{:S(2)}, u32[]{:S(2)}) collective-permute-start(bf16[4,128,1280]{2,1,0:T(8,128)(2,1)} %get-tuple-element.19), channel_id=1, source_target_pairs={{0,1},{1,0},{2,3},{3,2},{4,5},{5,4},{6,7},{7,6},{8,9},{9,8},{10,11... | collective-permute-start | bytes 3932168 | tf_op jit(solution)/shard_map/ppermute | solution.py:38
  33.6 75.9 %copy-start.6 = (bf16[1,128,2560]{2,1,0:T(8,128)(2,1)S(1)}, bf16[1,128,2560]{2,1,0:T(8,128)(2,1)}, u32[]{:S(2)}) copy-start(bf16[1,128,2560]{2,1,0:T(8,128)(2,1)} %q.3) | copy-start | bytes 1966084
  33.6 75.9 %copy-start.8 = (bf16[1,128,2560]{2,1,0:T(8,128)(2,1)S(1)}, bf16[1,128,2560]{2,1,0:T(8,128)(2,1)}, u32[]{:S(2)}) copy-start(bf16[1,128,2560]{2,1,0:T(8,128)(2,1)} %tq.3) | copy-start | bytes 1966084
  33.6 75.9 %collective-permute-start.2 = (bf16[4,128,1280]{2,1,0:T(8,128)(2,1)}, bf16[4,128,1280]{2,1,0:T(8,128)(2,1)}, u32[]{:S(2)}, u32[]{:S(2)}) collective-permute-start(bf16[4,128,1280]{2,1,0:T(8,128)(2,1)} %get-tuple-element.20), channel_id=1, source_target_pairs={{0,2},{1,3},{2,4},{3,5},{4,6},{5,7},{6,8},{7,9},{8,10},{9,11},{10,... | collective-permute-start | bytes 3932168 | tf_op jit(solution)/shard_map/ppermute | solution.py:38
  38.3 71.2 %collective-permute-start.3 = (bf16[4,128,1280]{2,1,0:T(8,128)(2,1)}, bf16[4,128,1280]{2,1,0:T(8,128)(2,1)}, u32[]{:S(2)}, u32[]{:S(2)}) collective-permute-start(bf16[4,128,1280]{2,1,0:T(8,128)(2,1)} %collective-permute-done.sib_kv), channel_id=1, source_target_pairs={{0,2},{1,3},{2,4},{3,5},{4,6},{5,7},{6,8},{7,9},{8,10},{9,11},{10,... | collective-permute-start | bytes 3932168 | tf_op jit(solution)/shard_map/ppermute | solution.py:38
  41.1 67.6 %copy-start.1 = (bf16[4,128,1280]{2,1,0:T(8,128)(2,1)}, bf16[4,128,1280]{2,1,0:T(8,128)(2,1)S(1)}, u32[]{:S(2)}) copy-start(bf16[4,128,1280]{2,1,0:T(8,128)(2,1)S(1)} %collective-permute-done.1.sib_q) | copy-start | bytes 3932164
  102.7 6.8 %copy-start.10 = (bf16[1,128,2560]{2,1,0:T(8,128)(2,1)S(1)}, bf16[1,128,2560]{2,1,0:T(8,128)(2,1)}, u32[]{:S(2)}) copy-start(bf16[1,128,2560]{2,1,0:T(8,128)(2,1)} %k.3) | copy-start | bytes 1966084
  102.7 6.8 %copy-start.12 = (bf16[1,128,2560]{2,1,0:T(8,128)(2,1)S(1)}, bf16[1,128,2560]{2,1,0:T(8,128)(2,1)}, u32[]{:S(2)}) copy-start(bf16[1,128,2560]{2,1,0:T(8,128)(2,1)} %tk.3) | copy-start | bytes 1966084
  102.7 6.8 %copy-start.14 = (bf16[1,128,2560]{2,1,0:T(8,128)(2,1)S(1)}, bf16[1,128,2560]{2,1,0:T(8,128)(2,1)}, u32[]{:S(2)}) copy-start(bf16[1,128,2560]{2,1,0:T(8,128)(2,1)} %v.3) | copy-start | bytes 1966084
  102.7 6.8 %copy-start.16 = (bf16[1,128,2560]{2,1,0:T(8,128)(2,1)S(1)}, bf16[1,128,2560]{2,1,0:T(8,128)(2,1)}, u32[]{:S(2)}) copy-start(bf16[1,128,2560]{2,1,0:T(8,128)(2,1)} %tv.3) | copy-start | bytes 1966084
  108.6 0.8 copy-start.2
  127.2 12.2 %collective-permute-start.5 = (bf16[3,128,1280]{2,1,0:T(8,128)(2,1)}, bf16[3,128,1280]{2,1,0:T(8,128)(2,1)S(1)}, u32[]{:S(2)}, u32[]{:S(2)}) collective-permute-start(bf16[3,128,1280]{2,1,0:T(8,128)(2,1)} %get-tuple-element.22), channel_id=1, source_target_pairs={{0,1},{1,0},{2,3},{3,2},{4,5},{5,4},{6,7},{7,6},{8,9},{9,8},{10,11... | collective-permute-start | bytes 2949128 | tf_op jit(solution)/shard_map/ppermute | solution.py:38
  127.9 11.6 %copy-start = (f32[3,128,1280]{2,1,0:T(8,128)S(1)}, f32[3,128,1280]{2,1,0:T(8,128)}, u32[]{:S(2)}) copy-start(f32[3,128,1280]{2,1,0:T(8,128)} %get-tuple-element.21.own) | copy-start | bytes 5898244
  133.6 5.9 %collective-permute-start.6 = (bf16[128,2560]{1,0:T(8,128)(2,1)S(1)}, bf16[128,2560]{1,0:T(8,128)(2,1)S(1)}, u32[]{:S(2)}, u32[]{:S(2)}) collective-permute-start(bf16[128,2560]{1,0:T(8,128)(2,1)S(1)} %get-tuple-element.25), channel_id=1, source_target_pairs={{0,1},{1,0},{2,3},{3,2},{4,5},{5,4},{6,7},{7,6},{8,9},{9,8},{10,11... | collective-permute-start | bytes 1966088 | tf_op jit(solution)/shard_map/ppermute | solution.py:38
  133.7 18.6 %collective-permute-start.7 = (bf16[2,128,1280]{2,1,0:T(8,128)(2,1)S(1)}, bf16[2,128,1280]{2,1,0:T(8,128)(2,1)S(1)}, u32[]{:S(2)}, u32[]{:S(2)}) collective-permute-start(bf16[2,128,1280]{2,1,0:T(8,128)(2,1)S(1)} %get-tuple-element.28), channel_id=1, source_target_pairs={{0,14},{1,15},{2,0},{3,1},{4,2},{5,3},{6,4},{7,5},{8,6},{9,7},{10,... | collective-permute-start | bytes 1966088 | tf_op jit(solution)/shard_map/ppermute | solution.py:38
  138.6 27.7 %collective-permute-start.8 = (bf16[2,128,1280]{2,1,0:T(8,128)(2,1)S(1)}, bf16[2,128,1280]{2,1,0:T(8,128)(2,1)S(1)}, u32[]{:S(2)}, u32[]{:S(2)}) collective-permute-start(bf16[2,128,1280]{2,1,0:T(8,128)(2,1)S(1)} %get-tuple-element.29), channel_id=1, source_target_pairs={{0,15},{1,14},{2,1},{3,0},{4,3},{5,2},{6,5},{7,4},{8,7},{9,6},{10,... | collective-permute-start | bytes 1966088 | tf_op jit(solution)/shard_map/ppermute | solution.py:38
Sparse Core Ops, SparseCore 0:
  23.1 79.5 all-gather.1

commit v3 on v0

v3 whole, which is shorter than its diff:
```python
import jax
import jax.numpy as jnp
from jax import lax
from jax.experimental import pallas as pl
from jax.experimental.pallas import tpu as pltpu
from jax.sharding import Mesh
from jax.sharding import PartitionSpec as P

HEADS = 20
HEAD_DIM = 128
ROWS = 128
WIDTH = HEADS * HEAD_DIM
HALF = WIDTH // 2
PART = WIDTH // 4
PART_HEADS = HEADS // 4
FACTOR = HEAD_DIM ** (-0.5)

AXES = ("yl", "z", "x", "yh", "c")
SIZES = (2, 8, 4, 2, 2)

F32 = jnp.float32
BF16 = jnp.bfloat16
VMEM_LIMIT = 60 * 1024 * 1024
SMALL_LIMIT = 28 * 1024 * 1024
COST = pl.CostEstimate(flops=10**10, bytes_accessed=10**7, transcendentals=0)


def permute(block, move):
    route = []
    for index in range(256):
        rest, place = index, []
        for size in reversed(SIZES):
            place.append(rest % size)
            rest //= size
        goal = 0
        for coordinate, size in zip(move(*reversed(place)), SIZES):
            goal = goal * size + coordinate
        route.append((index, goal))
    return lax.ppermute(block, AXES, route)


def to_chip(step, cross=False):
    def move(yl, z, x, yh, c):
        chip = (x * 2 + yh + step) % 8
        return yl, z, chip // 2, chip % 2, (1 - c if cross else c)

    return move


def to_sibling(yl, z, x, yh, c):
    return yl, z, x, yh, 1 - c


def to_pair(yl, z, x, yh, c):
    return yl, z, x ^ 1, yh, c


def swap_low_and_core(yl, z, x, yh, c):
    return c, z, x, yh, yl


def columns(part, width=PART):
    return pl.ds(pl.multiple_of(part * width, width), width)


def dot(a, b, dims):
    return lax.dot_general(a, b, (dims, ((), ())), preferred_element_type=F32)


NT = ((1,), (1,))
NN = ((1,), (0,))
TN = ((0,), (0,))
ANYWHERE = pl.BlockSpec(memory_space=pl.ANY)
SCALARS = pl.BlockSpec(memory_space=pltpu.SMEM)


def stacked(n):
    return jax.ShapeDtypeStruct((n, ROWS, PART), BF16)


def pack_call(kernel, name, inputs, outputs, *arrays):
    steps = 2
    tile = ROWS // steps

    def spec(n):
        if n is None:
            return ANYWHERE
        if n == 0:
            return pl.BlockSpec((1, tile, WIDTH), lambda i: (0, i, 0))
        return pl.BlockSpec((n, tile, PART), lambda i: (0, i, 0))

    return pl.pallas_call(
        kernel,
        grid=(steps,),
        out_shape=[stacked(n) for n in outputs],
        in_specs=[SCALARS] + [spec(n) for n in inputs],
        out_specs=[spec(n) for n in outputs],
        compiler_params=pltpu.CompilerParams(vmem_limit_bytes=VMEM_LIMIT),
        cost_estimate=COST,
        name=name,
    )(*arrays)


def pack_first_kernel(place, q, tq, k, tk, v, tv, cot, own, sib, pair):
    core, side = place[0], place[1]
    for entry, source in enumerate((k, tk, v, tv, q, tq)):
        if entry < 4:
            own[entry] = source[0, :, columns(2 * core)]
        sib[entry] = source[0, :, columns(2 - 2 * core)]
    for entry, source in enumerate((q, tq)):
        sib[6 + entry] = source[0, :, columns(3 - 2 * core)]
    for entry in range(2):
        sib[8 + entry] = cot[0, :, columns(2 * side + entry)]
        pair[entry] = cot[0, :, columns(2 - 2 * side + entry)]


def pack_second_kernel(place, k, tk, v, tv, near, far, sib):
    core = place[0]
    for entry, source in enumerate((k, tk, v, tv)):
        far[entry] = near[entry]
        far[4 + entry] = source[0, :, columns(2 * core + 1)]
        sib[entry] = source[0, :, columns(3 - 2 * core)]


def halves_kernel(place, shard, first, used, other):
    del first
    side = place[1]
    used[...] = shard[:, columns(side, HALF)]
    other[...] = shard[:, columns(1 - side, HALF)]


def halves(place, shard, first):
    whole = pl.BlockSpec(memory_space=pltpu.VMEM)
    out = jax.ShapeDtypeStruct((shard.shape[0], HALF), BF16)
    return pl.pallas_call(
        halves_kernel,
        out_shape=(out, out),
        in_specs=[SCALARS, whole, ANYWHERE],
        out_specs=(whole, whole),
        compiler_params=pltpu.CompilerParams(vmem_limit_bytes=SMALL_LIMIT),
        cost_estimate=COST,
        name="halves",
    )(place, shard, first)


def project_kernel(place, cot, near, pair, pair_near, weight, own, send0, send1, rows):
    del place
    step = pl.program_id(0)

    @pl.when(step == 0)
    def _():
        rows[:ROWS, :] = cot[0]
        for block, ref in enumerate((near, pair, pair_near)):
            start = (block + 1) * ROWS
            rows[start : start + ROWS, :PART] = ref[0]
            rows[start : start + ROWS, PART:] = ref[1]

    out = dot(rows[...], weight[...], NT)
    own[...] = out[: 2 * ROWS]
    for chunk, send in enumerate((send0, send1)):

        @pl.when(step == chunk)
        def _(send=send):
            send[...] = out[2 * ROWS :].astype(BF16)


def project(place, cot, near, pair, pair_near, weight):
    def stack(start):
        return pl.BlockSpec((2, ROWS, PART), lambda i, place: (start, 0, 0))

    block = pl.BlockSpec((2 * ROWS, PART), lambda i, place: (0, 0))
    send = jax.ShapeDtypeStruct((2 * ROWS, PART), BF16)
    return pl.pallas_call(
        project_kernel,
        out_shape=(jax.ShapeDtypeStruct((2 * ROWS, HALF), F32), send, send),
        grid_spec=pltpu.PrefetchScalarGridSpec(
            num_scalar_prefetch=1,
            grid=(2,),
            in_specs=[
                pl.BlockSpec((1, ROWS, HALF), lambda i, place: (0, 0, place[1])),
                stack(4),
                stack(0),
                stack(0),
                pl.BlockSpec((PART, HALF), lambda i, place: (i, 0)),
            ],
            out_specs=(
                pl.BlockSpec((2 * ROWS, PART), lambda i, place: (0, i)), block, block
            ),
            scratch_shapes=[pltpu.VMEM((4 * ROWS, HALF), BF16)],
        ),
        compiler_params=pltpu.CompilerParams(vmem_limit_bytes=SMALL_LIMIT),
        cost_estimate=COST,
        name="project",
    )(place, cot, near, pair, pair_near, weight)


def attend_head(core, chunk, head, refs):
    q, tq, k, tk, v, tv, near, near_q, far_own, far_sib, grad_own, grad_pair, *outs = refs
    own_q, own_kv, sib_out, back_own, back_sib, tan_out = outs
    start = head * HEAD_DIM
    cols = slice(start, start + HEAD_DIM)
    start += chunk * PART
    grad_cols = slice(start, start + HEAD_DIM)
    start += core * HALF
    raw = slice(start, start + HEAD_DIM)
    far_entry = 4 * chunk
    sib_far = 4 if chunk == 0 else 4

    def ordered(own, sib):
        return [own, sib] if core == 0 else [sib, own]

    def window(entry, source):
        blocks = ordered(far_own[far_entry + entry, :, cols], far_sib[entry, :, cols]) + ordered(
            source[0, :, raw], near[entry, :, cols]
        )
        return jnp.concatenate(blocks, axis=0)

    key, tkey, value, tvalue = (window(i, source) for i, source in enumerate((k, tk, v, tv)))
    query = ordered(q[0, :, raw], near_q[4 + 2 * chunk, :, cols])
    tquery = ordered(tq[0, :, raw], near_q[5 + 2 * chunk, :, cols])
    grad = (grad_own[:, grad_cols] + grad_pair[:, cols].astype(F32)).astype(BF16)
    grad = ordered(grad[:ROWS], grad[ROWS:])
    both_key = jnp.concatenate([key, tkey], axis=1)
    span = 3 * ROWS
    zero = jnp.zeros((ROWS, ROWS), BF16)
    probs, gss, tans, qgs = [], [], [], []
    for block in range(2):
        seen = slice(block * ROWS, block * ROWS + span)
        scores = dot(query[block], key[seen], NT)
        both_query = jnp.concatenate([tquery[block], query[block]], axis=1)
        tan_scores = dot(both_query, both_key[seen], NT)
        grad_prob = dot(grad[block], value[seen], NT)
        top = jnp.max(scores, axis=-1, keepdims=True)
        expos = jnp.exp((scores - top) * FACTOR)
        prob = expos * (1.0 / jnp.sum(expos, axis=-1, keepdims=True))
        prob_b = prob.astype(BF16)
        mean = jnp.sum(prob * tan_scores, axis=-1, keepdims=True)
        scaled = prob * FACTOR
        tan_prob = (scaled * (tan_scores - mean)).astype(BF16)
        delta = jnp.sum(prob_b.astype(F32) * grad_prob, axis=-1, keepdims=True)
        gs = (scaled * (grad_prob - delta)).astype(BF16)
        tans.append(dot(prob_b, tvalue[seen], NN) + dot(tan_prob, value[seen], NN))
        qgs.append(dot(gs, key[seen], NN))
        fill = [prob_b, zero] if block == 0 else [zero, prob_b]
        probs.append(jnp.concatenate(fill, axis=1))
        fill = [gs, zero] if block == 0 else [zero, gs]
        gss.append(jnp.concatenate(fill, axis=1))
    kg = dot(jnp.concatenate(gss, axis=0), jnp.concatenate(query, axis=0), TN)
    vg = dot(jnp.concatenate(probs, axis=0), jnp.concatenate(grad, axis=0), TN)

    def block_of(whole, index):
        return whole[index * ROWS : (index + 1) * ROWS]

    tan_out[:ROWS, cols] = tans[core].astype(BF16)
    tan_out[ROWS:, cols] = tans[1 - core].astype(BF16)
    own_q[0, :, cols] = qgs[core].astype(BF16)
    sib_out[0, :, cols] = qgs[1 - core].astype(BF16)
    for entry, terms in enumerate((kg, vg)):
        back_own[entry, :, cols] = block_of(terms, core).astype(BF16)
        back_sib[entry, :, cols] = block_of(terms, 1 - core).astype(BF16)
        own_kv[entry, :, cols] = block_of(terms, 2 + core)
        sib_out[1 + entry, :, cols] = block_of(terms, 3 - core).astype(BF16)


def attend(place, chunk, *arrays):
    def kernel(place, *refs):
        for core in range(2):

            @pl.when(place[0] == core)
            def _(core=core):
                for head in range(PART_HEADS):
                    attend_head(core, chunk, head, refs)

    whole = pl.BlockSpec(memory_space=pltpu.VMEM)

    def out(n, dtype):
        return jax.ShapeDtypeStruct((n, ROWS, PART), dtype)

    return pl.pallas_call(
        kernel,
        out_shape=(
            out(1, BF16), out(2, F32), out(3, BF16), out(2, BF16), out(2, BF16),
            jax.ShapeDtypeStruct((2 * ROWS, PART), BF16),
        ),
        in_specs=[SCALARS] + [whole] * len(arrays),
        out_specs=(whole,) * 6,
        compiler_params=pltpu.CompilerParams(vmem_limit_bytes=SMALL_LIMIT),
        cost_estimate=COST,
        name="attend",
    )(place, *arrays)


def tangent_kernel(place, tan0, tan1, weight0, weight1, back, cross, near, own, sib, total):
    del place, back, cross, near
    step = pl.program_id(0)
    for half, weight in enumerate((weight0, weight1)):

        @pl.when(step == 2 * half)
        def _(weight=weight):
            total[...] = dot(tan0[...], weight[...], NN)

        @pl.when(step == 2 * half + 1)
        def _(weight=weight):
            both = total[...] + dot(tan1[...], weight[...], NN)
            own[0] = both[:ROWS]
            sib[0] = both[ROWS:].astype(BF16)


def tangent(place, tan0, tan1, weight0, weight1, *earlier):
    whole = pl.BlockSpec((2 * ROWS, PART), lambda i, place: (0, 0))
    block = pl.BlockSpec((1, ROWS, HALF), lambda i, place: (i // 2, 0, 0))
    return pl.pallas_call(
        tangent_kernel,
        out_shape=(
            jax.ShapeDtypeStruct((2, ROWS, HALF), F32),
            jax.ShapeDtypeStruct((2, ROWS, HALF), BF16),
        ),
        grid_spec=pltpu.PrefetchScalarGridSpec(
            num_scalar_prefetch=1,
            grid=(4,),
            in_specs=[
                whole,
                whole,
                pl.BlockSpec((PART, HALF), lambda i, place: (jnp.minimum(i, 1), 0)),
                pl.BlockSpec((PART, HALF), lambda i, place: (jnp.maximum(i, 2) - 2, 0)),
            ]
            + [ANYWHERE] * len(earlier),
            out_specs=(block, block),
            scratch_shapes=[pltpu.VMEM((2 * ROWS, HALF), F32)],
        ),
        compiler_params=pltpu.CompilerParams(vmem_limit_bytes=SMALL_LIMIT),
        cost_estimate=COST,
        name="tangent",
    )(place, tan0, tan1, weight0, weight1, *earlier)


def finish_first_kernel(place, own0, own1, sib0, sib1, tan_own, tan_sib, q_out, tan_out):
    core, side = place[0], place[1]
    for chunk, (own, sib) in enumerate(((own0, sib0), (own1, sib1))):
        q_out[0, :, columns(2 * core + chunk)] = own[0]
        q_out[0, :, columns(2 - 2 * core + chunk)] = sib[0]
    for entry, half in enumerate((side, 1 - side)):
        tan_out[0, :, columns(half, HALF)] = (
            tan_own[entry] + tan_sib[entry].astype(F32)
        ).astype(BF16)


def finish_last_kernel(
    place, own0, own1, sib0, sib1, near0, near1, cross0, cross1, k_out, v_out
):
    core = place[0]
    chunks = ((own0, sib0, near0, cross0), (own1, sib1, near1, cross1))
    for chunk, (own, sib, near, cross) in enumerate(chunks):
        for entry, ref in enumerate((k_out, v_out)):
            ref[0, :, columns(2 * core + chunk)] = (
                own[entry] + near[entry].astype(F32)
            ).astype(BF16)
            ref[0, :, columns(2 - 2 * core + chunk)] = (
                sib[entry + 1].astype(F32) + cross[entry].astype(F32)
            ).astype(BF16)


def finish(kernel, name, place, *arrays):
    whole = pl.BlockSpec(memory_space=pltpu.VMEM)
    out = jax.ShapeDtypeStruct((1, ROWS, WIDTH), BF16)
    return pl.pallas_call(
        kernel,
        out_shape=(out, out),
        in_specs=[SCALARS] + [whole] * len(arrays),
        out_specs=(whole, whole),
        compiler_params=pltpu.CompilerParams(vmem_limit_bytes=SMALL_LIMIT),
        cost_estimate=COST,
        name=name,
    )(place, *arrays)


def body(q, k, v, tq, tk, tv, cot, out_weight):
    place = jnp.stack([lax.axis_index("c"), lax.axis_index("x") % 2]).astype(jnp.int32)
    arrays = (q, tq, k, tk, v, tv)

    shard = permute(out_weight, swap_low_and_core)
    own, sib, pair = pack_call(
        pack_first_kernel, "pack_first", [0] * 7, [4, 10, 2], place, *arrays, cot
    )
    near_0 = permute(sib, to_sibling)
    far_a = permute(own, to_chip(1))
    pair = permute(pair, to_pair)
    weight_a, weight_b = (
        lax.all_gather(half, "z", axis=0, tiled=True) for half in halves(place, shard, near_0)
    )
    far, sib = pack_call(
        pack_second_kernel, "pack_second", [0] * 4 + [10], [8, 4], place, k, tk, v, tv, near_0
    )
    near_1 = permute(sib, to_sibling)
    far_b = permute(far, to_chip(1))
    far_c = permute(near_1, to_chip(1))
    pair_near = permute(pair, to_sibling)

    grad, send_0, send_1 = project(place, cot, near_0, pair, pair_near, weight_a)
    grad_0 = permute(send_0, to_pair)
    grad_1 = permute(send_1, to_pair)

    def chunk_grads(chunk, *others):
        own_q, own_kv, sib, back_own, back_sib, tan = attend(place, chunk, *arrays, *others)
        back_own = permute(back_own, to_chip(-1))
        back_sib = permute(back_sib, to_chip(-1, cross=True))
        return own_q, own_kv, permute(sib, to_sibling), back_own, back_sib, tan

    q0, kv0, sib0, back0, cross0, tan0 = chunk_grads(
        0, near_0, near_0, far_a, far_b, grad, grad_0
    )
    q1, kv1, sib1, back1, cross1, tan1 = chunk_grads(
        1, near_1, near_0, far_b, far_c, grad, grad_1
    )
    tan_own, tan_sib = tangent(
        place, tan0, tan1, weight_a, weight_b, back0, cross0, sib0
    )
    tan_sib = permute(tan_sib, to_sibling)
    query_grad, tangent_out = finish(
        finish_first_kernel, "finish_first", place, q0, q1, sib0, sib1, tan_own, tan_sib
    )
    key_grad, value_grad = finish(
        finish_last_kernel, "finish_last", place,
        kv0, kv1, sib0, sib1, back0, back1, cross0, cross1,
    )
    return tangent_out, query_grad, key_grad, value_grad


def solution(mesh):
    cut = Mesh(mesh.devices.reshape(SIZES), AXES)
    rows = P(("yl", "z"), ("x", "yh", "c"), None)
    return jax.shard_map(
        body,
        mesh=cut,
        in_specs=(rows,) * 7 + (P(("yl", "z"), None),),
        out_specs=(rows,) * 4,
        check_vma=False,
    )
```

time: 342 us -> 160 us (0.47)
  waiting for transfers between devices: 203 us -> 60.4 us
  matrix products: 43.2 us -> 0 us
  Pallas kernels: 0 us -> 37.1 us
  local copies, waits for them, and re-layouts: 47.1 us -> 15.7 us
  other arithmetic: 5.18 us -> 0.62 us
    ppermute x12 -> x17, waiting for transfers between devices: 202 us -> 27.1 us  [permute(): return lax.ppermute(block, AXES, route)]
    dot_general x11 -> x0, matrix products: 40 us -> none  [the longest x1 8.98 us: body(): jnp.einsum('io,ao->ia', grad_out, full_weight, preferred_element_type=jnp...]
    pallas_call x0 -> x9, Pallas kernels: none -> 37.1 us  [the longest x2 16.9 us: attend(): pl.pallas_call(kernel, out_shape=(out(1, BF16), out(2, F32), out(3, BF16)...]
    all_gather x1 -> x2, waiting for transfers between devices: 0.01 us -> 32.6 us  [body(): lax.all_gather(half, 'z', axis=0, tiled=True)]
    slice x8 -> x0, local copies, waits for them, and re-layouts: 16.4 us -> none  [the longest x2 6.92 us: body(): value_terms[rows:2 * rows]]
    concatenate x6 -> x0, local copies, waits for them, and re-layouts: 9.04 us -> none  [the longest x3 5.89 us: body(): tk_window = jnp.concatenate([far_blocks[2], near_blocks[2], tk_own], axis=0)]
    ppermute x4 -> x0, local copies, waits for them, and re-layouts: 8.69 us -> none  [from_behind(): return lax.ppermute(block, axis, route)]
    broadcast_in_dim x2 -> x0, other arithmetic: 5.18 us -> none  [the longest x1 2.76 us: body(): key_grad[None]]
  transfers between devices with their start and end apart: 13 -> 19, of which waited for: 8 -> 5; matrix products, arithmetic and copies ran while one was open for 20% -> 0% of each run, Pallas kernels for 0% -> 19%
where the time goes in v3:
time: 160 us; the launch traced here: 159 us
  waiting for transfers between devices  60.4 us (38%)
  Pallas kernels  37.1 us (23%)
  starting transfers between devices  30.9 us (19%)
  local copies, waits for them, and re-layouts  15.7 us (10%)
  between operations  14.3 us (9%)
    all_gather x2, waiting for transfers between devices, body(): lax.all_gather(half, 'z', axis=0, tiled=True)  32.6 us
    ppermute x17, starting transfers between devices, permute(): return lax.ppermute(block, AXES, route)  30.9 us
    ppermute x17, waiting for transfers between devices, permute(): return lax.ppermute(block, AXES, route)  27.1 us
    pallas_call x2, Pallas kernels, attend(): pl.pallas_call(kernel, out_shape=(out(1, BF16), out(2, F32), out(3, BF16)...  16.9 us
    unnamed x68, local copies, waits for them, and re-layouts  15.7 us
    pallas_call x2, Pallas kernels, pack_call(): pl.pallas_call(kernel, grid=(steps,), out_shape=[stacked(n) for n in outp...  6.75 us
    pallas_call x2, Pallas kernels, finish(): pl.pallas_call(kernel, out_shape=(out, out), in_specs=[SCALARS] + [whole]...  5.17 us
    pallas_call x1, Pallas kernels, tangent(): pl.pallas_call(tangent_kernel, out_shape=(jax.ShapeDtypeStruct((2, ROWS,...  3.41 us
  transfers between devices with their start and end apart: 19, of which 5 were waited for; matrix products, arithmetic and copies ran while one was open for 0% of the time, Pallas kernels for 19%

profile of v3, /device:TPU:1, one launch (start us, length us, event | category | flops | bytes accessed | tf_op | source)
XLA Modules:
  0.0 159.1 jit_solution(1271483232571586912)
XLA Ops:
  7.2 0.0 all-gather.3.cloned.1.call-start
  7.2 0.6 pad_add_fusion.place
  7.8 3.5 %pack_first.1 = (bf16[4,128,640]{2,1,0:T(8,128)(2,1)}, bf16[10,128,640]{2,1,0:T(8,128)(2,1)}, bf16[2,128,640]{2,1,0:T(8,128)(2,1)}) custom-call(s32[2]{0:T(128)} %pad_add_fusion.place, bf16[1,128,2560]{2,1,0:T(8,128)(2,1)} %refs_0_.3, bf16[1,128,2560]{2,1,0:T(8,128)(2,1)} %refs_1_.3, bf16[1,128,2560]{2,1,0:T(8,128)(2,1)} %refs_2_.3, ...), custom_call_target="tpu_custom_call" | custom-call | flops 10000000000 | bytes 10000000 | tf_op jit(solution)/shard_map/pack_first/pallas_call | solution.py:92
  11.4 3.3 %collective-permute-start = (bf16[10,128,640]{2,1,0:T(8,128)(2,1)}, bf16[10,128,640]{2,1,0:T(8,128)(2,1)S(1)}, u32[]{:S(2)}, u32[]{:S(2)}) collective-permute-start(bf16[10,128,640]{2,1,0:T(8,128)(2,1)} %get-tuple-element.32), channel_id=1, source_target_pairs={{0,1},{1,0},{2,3},{3,2},{4,5},{5,4},{6,7},{7,6},{8,9},{9,8},{10,11... | collective-permute-start | bytes 4915208 | tf_op jit(solution)/shard_map/ppermute | solution.py:39
  14.7 1.9 %collective-permute-start.5 = (bf16[160,2560]{1,0:T(8,128)(2,1)S(1)}, bf16[160,2560]{1,0:T(8,128)(2,1)S(1)}, u32[]{:S(2)}, u32[]{:S(2)}) collective-permute-start(bf16[160,2560]{1,0:T(8,128)(2,1)S(1)} %copy-done.32), channel_id=1, source_target_pairs={{0,0},{1,128},{2,2},{3,130},{4,4},{5,132},{6,6},{7,134},{8,8},{9,1... | collective-permute-start | bytes 2457608 | tf_op jit(solution)/shard_map/ppermute | solution.py:39
  16.6 11.7 %collective-permute-done.5.shard = bf16[160,2560]{1,0:T(8,128)(2,1)S(1)} collective-permute-done((bf16[160,2560]{1,0:T(8,128)(2,1)S(1)}, bf16[160,2560]{1,0:T(8,128)(2,1)S(1)}, u32[]{:S(2)}, u32[]{:S(2)}) %collective-permute-start.5) | collective-permute-done | bytes 819232 | tf_op jit(solution)/shard_map/ppermute | solution.py:39
  28.3 0.0 collective-permute-done.near.first.refs_6_.refs_7_
  28.3 1.5 halves.1
  29.9 0.0 all-gather.3.cloned.1.call-update
  29.9 0.0 all-gather.5.cloned.1.call-start
  30.0 0.7 all-gather.5.cloned.1.call-update
  30.7 0.1 collective-permute-start.3
  30.8 5.9 %collective-permute-done.3.pair = bf16[2,128,640]{2,1,0:T(8,128)(2,1)S(1)} collective-permute-done((bf16[2,128,640]{2,1,0:T(8,128)(2,1)S(1)}, bf16[2,128,640]{2,1,0:T(8,128)(2,1)S(1)}, u32[]{:S(2)}, u32[]{:S(2)}) %collective-permute-start.3) | collective-permute-done | bytes 327712 | tf_op jit(solution)/shard_map/ppermute | solution.py:39
  36.7 0.0 collective-permute-start.4
  36.7 3.2 %pack_second.1 = (bf16[8,128,640]{2,1,0:T(8,128)(2,1)}, bf16[4,128,640]{2,1,0:T(8,128)(2,1)}) custom-call(s32[2]{0:T(128)} %pad_add_fusion.place, bf16[1,128,2560]{2,1,0:T(8,128)(2,1)} %refs_2_.3, bf16[1,128,2560]{2,1,0:T(8,128)(2,1)} %refs_3_.3, bf16[1,128,2560]{2,1,0:T(8,128)(2,1)} %refs_4_.3, bf16[1,128,2560]{2,1,0:T(8,128)(2,1)} %refs_5_.3, ...), custom_call_target="tpu_custom_call" | custom-call | flops 10000000000 | bytes 10000000 | tf_op jit(solution)/shard_map/pack_second/pallas_call | solution.py:92
  40.0 1.2 collective-permute-start.2
  41.1 1.5 collective-permute-start.1
  42.7 1.1 collective-permute-start.7
  43.7 0.0 collective-permute-done.4.pair_near
  43.7 0.7 copy-done.18
  44.4 32.6 %all-gather.3.cloned.1.call-done.weight.weight0 = bf16[1280,1280]{1,0:T(8,128)(2,1)} async-done(((bf16[160,1280]{1,0:T(8,128)(2,1)}), bf16[1280,1280]{1,0:T(8,128)(2,1)}) %all-gather.3.cloned.1.call-update) | async-done | bytes 3276816 | tf_op jit(solution)/shard_map/all_gather | solution.py:389
  77.0 1.9 %copy-done = bf16[1280,1280]{1,0:T(8,128)(2,1)S(1)} copy-done((bf16[1280,1280]{1,0:T(8,128)(2,1)S(1)}, bf16[1280,1280]{1,0:T(8,128)(2,1)}, u32[]{:S(2)}) %copy-start) | copy-done | bytes 3276824
  78.9 1.1 copy-done.8
  80.0 1.0 copy-done.19
  81.0 0.0 copy-start.13
  81.0 0.0 copy-start.14
  81.0 3.3 %project.1 = (f32[256,1280]{1,0:T(8,128)S(1)}, bf16[256,640]{1,0:T(8,128)(2,1)S(1)}, bf16[256,640]{1,0:T(8,128)(2,1)S(1)}) custom-call(s32[2]{0:T(128)S(1)} %copy-done.21, bf16[1,128,2560]{2,1,0:T(8,128)(2,1)S(1)} %copy-done.8, bf16[10,128,640]{2,1,0:T(8,128)(2,1)S(1)} %copy-done.4, bf16[2,128,640]{2,1,0:T(8,128)(2,1)S(1)} %collective-permute-done.3.pair, ...), custom_call_target="tpu_custom_call" | custom-call | flops 10000000000 | bytes 10000000 | tf_op jit(solution)/shard_map/project/pallas_call | solution.py:173
  84.4 1.3 collective-permute-start.6
  85.6 0.0 collective-permute-done.7.refs_6_
  85.6 2.7 %collective-permute-start.8 = (bf16[4,128,640]{2,1,0:T(8,128)(2,1)}, bf16[4,128,640]{2,1,0:T(8,128)(2,1)S(1)}, u32[]{:S(2)}, u32[]{:S(2)}) collective-permute-start(bf16[4,128,640]{2,1,0:T(8,128)(2,1)} %collective-permute-done.7.refs_6_), channel_id=1, source_target_pairs={{0,2},{1,3},{2,4},{3,5},{4,6},{5,7},{6,8},{7,9},{8,10},{9,11},{10,... | collective-permute-start | bytes 1966088 | tf_op jit(solution)/shard_map/ppermute | solution.py:39
  88.4 0.3 collective-permute-start.9
  88.6 0.0 collective-permute-done.1.refs_8_
  88.6 0.0 collective-permute-done.2.refs_9_.refs_8_
  88.7 4.5 %collective-permute-done.6.refs_11_ = bf16[256,640]{1,0:T(8,128)(2,1)S(1)} collective-permute-done((bf16[256,640]{1,0:T(8,128)(2,1)S(1)}, bf16[256,640]{1,0:T(8,128)(2,1)S(1)}, u32[]{:S(2)}, u32[]{:S(2)}) %collective-permute-start.6) | collective-permute-done | bytes 327712 | tf_op jit(solution)/shard_map/ppermute | solution.py:39
  93.2 8.5 %attend.2 = (bf16[1,128,640]{2,1,0:T(8,128)(2,1)S(1)}, f32[2,128,640]{2,1,0:T(8,128)S(1)}, bf16[3,128,640]{2,1,0:T(8,128)(2,1)}, bf16[2,128,640]{2,1,0:T(8,128)(...) custom-call(s32[2]{0:T(128)S(1)} %copy-done.21, bf16[1,128,2560]{2,1,0:T(8,128)(2,1)S(1)} %copy-done.9, ...), custom_call_target="tpu_custom_call" | custom-call | flops 10000000000 | bytes 10000000 | tf_op jit(solution)/shard_map/attend/pallas_call | solution.py:279
  101.7 0.8 copy-done.22
  102.5 0.7 copy-done.26
  103.2 2.6 %collective-permute-start.10 = (bf16[3,128,640]{2,1,0:T(8,128)(2,1)}, bf16[3,128,640]{2,1,0:T(8,128)(2,1)}, u32[]{:S(2)}, u32[]{:S(2)}) collective-permute-start(bf16[3,128,640]{2,1,0:T(8,128)(2,1)} %get-tuple-element.43), channel_id=1, source_target_pairs={{0,1},{1,0},{2,3},{3,2},{4,5},{5,4},{6,7},{7,6},{8,9},{9,8},{10,11... | collective-permute-start | bytes 1474568 | tf_op jit(solution)/shard_map/ppermute | solution.py:39
  105.8 4.9 %collective-permute-start.12 = (bf16[2,128,640]{2,1,0:T(8,128)(2,1)S(1)}, bf16[2,128,640]{2,1,0:T(8,128)(2,1)S(1)}, u32[]{:S(2)}, u32[]{:S(2)}) collective-permute-start(bf16[2,128,640]{2,1,0:T(8,128)(2,1)S(1)} %get-tuple-element.48), channel_id=1, source_target_pairs={{0,14},{1,15},{2,0},{3,1},{4,2},{5,3},{6,4},{7,5},{8,6},{9,7},{10,... | collective-permute-start | bytes 983048 | tf_op jit(solution)/shard_map/ppermute | solution.py:39
  110.7 0.4 collective-permute-start.13
  111.1 0.0 collective-permute-done.8.refs_9_
  111.1 0.0 collective-permute-done.9.refs_11_
  111.1 1.6 copy-done.7
  112.7 8.5 %attend.3 = (bf16[1,128,640]{2,1,0:T(8,128)(2,1)S(1)}, f32[2,128,640]{2,1,0:T(8,128)S(1)}, bf16[3,128,640]{2,1,0:T(8,128)(2,1)}, bf16[2,128,640]{2,1,0:T(8,128)(...) custom-call(s32[2]{0:T(128)S(1)} %copy-done.21, bf16[1,128,2560]{2,1,0:T(8,128)(2,1)S(1)} %copy-done.9, ...), custom_call_target="tpu_custom_call" | custom-call | flops 10000000000 | bytes 10000000 | tf_op jit(solution)/shard_map/attend/pallas_call | solution.py:279
  121.1 0.8 copy-done.24
  122.0 0.7 copy-done.28
  122.7 0.6 copy-done.30
  123.4 0.2 collective-permute-start.11
  123.6 9.0 %collective-permute-start.15 = (bf16[2,128,640]{2,1,0:T(8,128)(2,1)}, bf16[2,128,640]{2,1,0:T(8,128)(2,1)}, u32[]{:S(2)}, u32[]{:S(2)}) collective-permute-start(bf16[2,128,640]{2,1,0:T(8,128)(2,1)} %get-tuple-element.56), channel_id=1, source_target_pairs={{0,14},{1,15},{2,0},{3,1},{4,2},{5,3},{6,4},{7,5},{8,6},{9,7},{10,... | collective-permute-start | bytes 983048 | tf_op jit(solution)/shard_map/ppermute | solution.py:39
  132.5 0.0 collective-permute-done.12.back.near0
  132.5 0.7 copy-done.15
  133.3 0.0 collective-permute-start.16
  133.3 0.0 collective-permute-done.13.cross.cross0
  133.3 1.9 %copy-done.2 = bf16[1280,1280]{1,0:T(8,128)(2,1)S(1)} copy-done((bf16[1280,1280]{1,0:T(8,128)(2,1)S(1)}, bf16[1280,1280]{1,0:T(8,128)(2,1)}, u32[]{:S(2)}) %copy-start.2) | copy-done | bytes 3276824
  135.2 1.0 copy-done.16
  136.2 1.0 copy-done.27
  137.2 1.0 copy-done.29
  138.2 3.4 %tangent.1 = (f32[2,128,1280]{2,1,0:T(8,128)S(1)}, bf16[2,128,1280]{2,1,0:T(8,128)(2,1)S(1)}) custom-call(s32[2]{0:T(128)S(1)} %copy-done.21, bf16[256,640]{1,0:T(8,128)(2,1)S(1)} %copy-done.27, bf16[256,640]{1,0:T(8,128)(2,1)S(1)} %copy-done.29, bf16[1280,1280]{1,0:T(8,128)(2,1)S(1)} %copy-done.1, bf16[1280,1280]{1,0:T(8,128)(2,1)S(1)} %copy-done.2, ...), custom_call_target="tpu_custom_call" | custom-call | flops 10000000000 | bytes 10000000 | tf_op jit(solution)/shard_map/tangent/pallas_call | solution.py:312
  141.6 0.5 collective-permute-start.14
  142.0 0.0 collective-permute-done.15.near1
  142.0 5.0 %collective-permute-done.16.cross1 = bf16[2,128,640]{2,1,0:T(8,128)(2,1)} collective-permute-done((bf16[2,128,640]{2,1,0:T(8,128)(2,1)}, bf16[2,128,640]{2,1,0:T(8,128)(2,1)}, u32[]{:S(2)}, u32[]{:S(2)}) %collective-permute-start.16) | collective-permute-done | bytes 327712 | tf_op jit(solution)/shard_map/ppermute | solution.py:39
  147.0 2.8 %finish_last.1 = (bf16[1,128,2560]{2,1,0:T(8,128)(2,1)}, bf16[1,128,2560]{2,1,0:T(8,128)(2,1)}) custom-call(s32[2]{0:T(128)S(1)} %copy-done.21, f32[2,128,640]{2,1,0:T(8,128)S(1)} %copy-done.23, f32[2,128,640]{2,1,0:T(8,128)S(1)} %copy-done.25, bf16[3,128,640]{2,1,0:T(8,128)(2,1)} %collective-permute-done.10.near.sib0, ...), custom_call_target="tpu_custom_call" | custom-call | flops 10000000000 | bytes 10000000 | tf_op jit(solution)/shard_map/finish_last/pallas_call | solution.py:366
  149.8 0.0 collective-permute-done.14.tan_sib
  149.8 2.4 %finish_first.1 = (bf16[1,128,2560]{2,1,0:T(8,128)(2,1)}, bf16[1,128,2560]{2,1,0:T(8,128)(2,1)}) custom-call(s32[2]{0:T(128)S(1)} %copy-done.21, bf16[1,128,640]{2,1,0:T(8,128)(2,1)S(1)} %get-tuple-element.39.own0, bf16[1,128,640]{2,1,0:T(8,128)(2,1)S(1)} %copy-done.31, bf16[3,128,640]{2,1,0:T(8,128)(2,1)} %collective-permute-done.10.near.sib0, ...), custom_call_target="tpu_custom_call" | custom-call | flops 10000000000 | bytes 10000000 | tf_op jit(solution)/shard_map/finish_first/pallas_call | solution.py:366
  (54 shorter events, 0.1 us)
Async XLA Ops:
  7.2 69.8 %all-gather.3.cloned.1.call-start = ((), (), s32[]{:S(2)}) async-start(), calls=%async_computation | async-start | bytes 3686400 | tf_op jit(solution)/shard_map/all_gather | solution.py:389
  7.8 6.8 %copy-start.32 = (bf16[160,2560]{1,0:T(8,128)(2,1)S(1)}, bf16[160,2560]{1,0:T(8,128)(2,1)}, u32[]{:S(2)}) copy-start(bf16[160,2560]{1,0:T(8,128)(2,1)} %param.15) | copy-start | bytes 2457604
  7.8 20.5 %copy-start.20 = (s32[2]{0:T(128)S(1)}, s32[2]{0:T(128)}, u32[]{:S(2)}) copy-start(s32[2]{0:T(128)} %pad_add_fusion.place) | copy-start | bytes 28
  11.3 19.3 %copy-start.33 = (bf16[2,128,640]{2,1,0:T(8,128)(2,1)S(1)}, bf16[2,128,640]{2,1,0:T(8,128)(2,1)}, u32[]{:S(2)}) copy-start(bf16[2,128,640]{2,1,0:T(8,128)(2,1)} %get-tuple-element.35) | copy-start | bytes 983044
  11.4 17.0 %collective-permute-start = (bf16[10,128,640]{2,1,0:T(8,128)(2,1)}, bf16[10,128,640]{2,1,0:T(8,128)(2,1)S(1)}, u32[]{:S(2)}, u32[]{:S(2)}) collective-permute-start(bf16[10,128,640]{2,1,0:T(8,128)(2,1)} %get-tuple-element.32), channel_id=1, source_target_pairs={{0,1},{1,0},{2,3},{3,2},{4,5},{5,4},{6,7},{7,6},{8,9},{9,8},{10,11... | collective-permute-start | bytes 4915208 | tf_op jit(solution)/shard_map/ppermute | solution.py:39
  14.7 13.6 %collective-permute-start.5 = (bf16[160,2560]{1,0:T(8,128)(2,1)S(1)}, bf16[160,2560]{1,0:T(8,128)(2,1)S(1)}, u32[]{:S(2)}, u32[]{:S(2)}) collective-permute-start(bf16[160,2560]{1,0:T(8,128)(2,1)S(1)} %copy-done.32), channel_id=1, source_target_pairs={{0,0},{1,128},{2,2},{3,130},{4,4},{5,132},{6,6},{7,134},{8,8},{9,1... | collective-permute-start | bytes 2457608 | tf_op jit(solution)/shard_map/ppermute | solution.py:39
  28.3 1.6 copy-start.3
  29.9 103.4 %all-gather.5.cloned.1.call-start = ((), (), s32[]{:S(2)}) async-start(), calls=%async_computation.1 | async-start | bytes 3686400 | tf_op jit(solution)/shard_map/all_gather | solution.py:389
  30.7 46.3 %copy-start.4 = (bf16[10,128,640]{2,1,0:T(8,128)(2,1)S(1)}, bf16[10,128,640]{2,1,0:T(8,128)(2,1)}, u32[]{:S(2)}) copy-start(bf16[10,128,640]{2,1,0:T(8,128)(2,1)} %copy-done.3) | copy-start | bytes 4915204
  30.7 46.3 %copy-start.21 = (s32[2]{0:T(128)S(1)}, s32[2]{0:T(128)}, u32[]{:S(2)}) copy-start(s32[2]{0:T(128)} %pad_add_fusion.place) | copy-start | bytes 28
  30.7 6.0 %collective-permute-start.3 = (bf16[2,128,640]{2,1,0:T(8,128)(2,1)S(1)}, bf16[2,128,640]{2,1,0:T(8,128)(2,1)S(1)}, u32[]{:S(2)}, u32[]{:S(2)}) collective-permute-start(bf16[2,128,640]{2,1,0:T(8,128)(2,1)S(1)} %copy-done.33), channel_id=1, source_target_pairs={{0,4},{1,5},{2,6},{3,7},{4,0},{5,1},{6,2},{7,3},{8,12},{9,13},{10,... | collective-permute-start | bytes 983048 | tf_op jit(solution)/shard_map/ppermute | solution.py:39
  36.7 7.0 %collective-permute-start.4 = (bf16[2,128,640]{2,1,0:T(8,128)(2,1)S(1)}, bf16[2,128,640]{2,1,0:T(8,128)(2,1)S(1)}, u32[]{:S(2)}, u32[]{:S(2)}) collective-permute-start(bf16[2,128,640]{2,1,0:T(8,128)(2,1)S(1)} %collective-permute-done.3.pair), channel_id=1, source_target_pairs={{0,1},{1,0},{2,3},{3,2},{4,5},{5,4},{6,7},{7,6},{8,9},{9,8},{10,11... | collective-permute-start | bytes 983048 | tf_op jit(solution)/shard_map/ppermute | solution.py:39
  40.0 48.7 %collective-permute-start.2 = (bf16[8,128,640]{2,1,0:T(8,128)(2,1)}, bf16[8,128,640]{2,1,0:T(8,128)(2,1)S(1)}, u32[]{:S(2)}, u32[]{:S(2)}) collective-permute-start(bf16[8,128,640]{2,1,0:T(8,128)(2,1)} %get-tuple-element.34), channel_id=1, source_target_pairs={{0,2},{1,3},{2,4},{3,5},{4,6},{5,7},{6,8},{7,9},{8,10},{9,11},{10,... | collective-permute-start | bytes 3932168 | tf_op jit(solution)/shard_map/ppermute | solution.py:39
  41.1 47.5 %collective-permute-start.1 = (bf16[4,128,640]{2,1,0:T(8,128)(2,1)}, bf16[4,128,640]{2,1,0:T(8,128)(2,1)}, u32[]{:S(2)}, u32[]{:S(2)}) collective-permute-start(bf16[4,128,640]{2,1,0:T(8,128)(2,1)} %get-tuple-element.33), channel_id=1, source_target_pairs={{0,2},{1,3},{2,4},{3,5},{4,6},{5,7},{6,8},{7,9},{8,10},{9,11},{10,... | collective-permute-start | bytes 1966088 | tf_op jit(solution)/shard_map/ppermute | solution.py:39
  42.7 43.0 %collective-permute-start.7 = (bf16[4,128,640]{2,1,0:T(8,128)(2,1)}, bf16[4,128,640]{2,1,0:T(8,128)(2,1)}, u32[]{:S(2)}, u32[]{:S(2)}) collective-permute-start(bf16[4,128,640]{2,1,0:T(8,128)(2,1)} %get-tuple-element.40), channel_id=1, source_target_pairs={{0,1},{1,0},{2,3},{3,2},{4,5},{5,4},{6,7},{7,6},{8,9},{9,8},{10,11... | collective-permute-start | bytes 1966088 | tf_op jit(solution)/shard_map/ppermute | solution.py:39
  43.7 0.7 copy-start.18
  77.0 1.9 %copy-start = (bf16[1280,1280]{1,0:T(8,128)(2,1)S(1)}, bf16[1280,1280]{1,0:T(8,128)(2,1)}, u32[]{:S(2)}) copy-start(bf16[1280,1280]{1,0:T(8,128)(2,1)} %all-gather.3.cloned.1.call-done.weight.weight0) | copy-start | bytes 9830404
  78.9 1.1 copy-start.8
  80.0 1.0 copy-start.19
  81.0 12.1 %copy-start.9 = (bf16[1,128,2560]{2,1,0:T(8,128)(2,1)S(1)}, bf16[1,128,2560]{2,1,0:T(8,128)(2,1)}, u32[]{:S(2)}) copy-start(bf16[1,128,2560]{2,1,0:T(8,128)(2,1)} %refs_0_.3) | copy-start | bytes 1966084
  81.0 12.1 %copy-start.10 = (bf16[1,128,2560]{2,1,0:T(8,128)(2,1)S(1)}, bf16[1,128,2560]{2,1,0:T(8,128)(2,1)}, u32[]{:S(2)}) copy-start(bf16[1,128,2560]{2,1,0:T(8,128)(2,1)} %refs_1_.3) | copy-start | bytes 1966084
  81.0 12.1 %copy-start.11 = (bf16[1,128,2560]{2,1,0:T(8,128)(2,1)S(1)}, bf16[1,128,2560]{2,1,0:T(8,128)(2,1)}, u32[]{:S(2)}) copy-start(bf16[1,128,2560]{2,1,0:T(8,128)(2,1)} %refs_2_.3) | copy-start | bytes 1966084
  81.0 12.1 %copy-start.12 = (bf16[1,128,2560]{2,1,0:T(8,128)(2,1)S(1)}, bf16[1,128,2560]{2,1,0:T(8,128)(2,1)}, u32[]{:S(2)}) copy-start(bf16[1,128,2560]{2,1,0:T(8,128)(2,1)} %refs_3_.3) | copy-start | bytes 1966084
  81.0 12.1 %copy-start.13 = (bf16[1,128,2560]{2,1,0:T(8,128)(2,1)S(1)}, bf16[1,128,2560]{2,1,0:T(8,128)(2,1)}, u32[]{:S(2)}) copy-start(bf16[1,128,2560]{2,1,0:T(8,128)(2,1)} %refs_4_.3) | copy-start | bytes 1966084
  81.0 12.1 %copy-start.14 = (bf16[1,128,2560]{2,1,0:T(8,128)(2,1)S(1)}, bf16[1,128,2560]{2,1,0:T(8,128)(2,1)}, u32[]{:S(2)}) copy-start(bf16[1,128,2560]{2,1,0:T(8,128)(2,1)} %refs_5_.3) | copy-start | bytes 1966084
  84.4 8.8 %collective-permute-start.6 = (bf16[256,640]{1,0:T(8,128)(2,1)S(1)}, bf16[256,640]{1,0:T(8,128)(2,1)S(1)}, u32[]{:S(2)}, u32[]{:S(2)}) collective-permute-start(bf16[256,640]{1,0:T(8,128)(2,1)S(1)} %get-tuple-element.38), channel_id=1, source_target_pairs={{0,4},{1,5},{2,6},{3,7},{4,0},{5,1},{6,2},{7,3},{8,12},{9,13},{10,... | collective-permute-start | bytes 983048 | tf_op jit(solution)/shard_map/ppermute | solution.py:39
  85.6 25.5 %collective-permute-start.8 = (bf16[4,128,640]{2,1,0:T(8,128)(2,1)}, bf16[4,128,640]{2,1,0:T(8,128)(2,1)S(1)}, u32[]{:S(2)}, u32[]{:S(2)}) collective-permute-start(bf16[4,128,640]{2,1,0:T(8,128)(2,1)} %collective-permute-done.7.refs_6_), channel_id=1, source_target_pairs={{0,2},{1,3},{2,4},{3,5},{4,6},{5,7},{6,8},{7,9},{8,10},{9,11},{10,... | collective-permute-start | bytes 1966088 | tf_op jit(solution)/shard_map/ppermute | solution.py:39
  88.4 22.7 %collective-permute-start.9 = (bf16[256,640]{1,0:T(8,128)(2,1)S(1)}, bf16[256,640]{1,0:T(8,128)(2,1)S(1)}, u32[]{:S(2)}, u32[]{:S(2)}) collective-permute-start(bf16[256,640]{1,0:T(8,128)(2,1)S(1)} %get-tuple-element.41), channel_id=1, source_target_pairs={{0,4},{1,5},{2,6},{3,7},{4,0},{5,1},{6,2},{7,3},{8,12},{9,13},{10,... | collective-permute-start | bytes 983048 | tf_op jit(solution)/shard_map/ppermute | solution.py:39
  88.7 13.0 %copy-start.6 = (bf16[8,128,640]{2,1,0:T(8,128)(2,1)}, bf16[8,128,640]{2,1,0:T(8,128)(2,1)S(1)}, u32[]{:S(2)}) copy-start(bf16[8,128,640]{2,1,0:T(8,128)(2,1)S(1)} %collective-permute-done.2.refs_9_.refs_8_) | copy-start | bytes 3932164
  93.2 17.9 %copy-start.5 = (bf16[10,128,640]{2,1,0:T(8,128)(2,1)S(1)}, bf16[10,128,640]{2,1,0:T(8,128)(2,1)}, u32[]{:S(2)}) copy-start(bf16[10,128,640]{2,1,0:T(8,128)(2,1)} %copy-done.3) | copy-start | bytes 4915204
  101.7 0.8 copy-start.22
  102.5 0.7 copy-start.26
  103.2 30.0 %collective-permute-start.10 = (bf16[3,128,640]{2,1,0:T(8,128)(2,1)}, bf16[3,128,640]{2,1,0:T(8,128)(2,1)}, u32[]{:S(2)}, u32[]{:S(2)}) collective-permute-start(bf16[3,128,640]{2,1,0:T(8,128)(2,1)} %get-tuple-element.43), channel_id=1, source_target_pairs={{0,1},{1,0},{2,3},{3,2},{4,5},{5,4},{6,7},{7,6},{8,9},{9,8},{10,11... | collective-permute-start | bytes 1474568 | tf_op jit(solution)/shard_map/ppermute | solution.py:39
  105.8 26.7 %collective-permute-start.12 = (bf16[2,128,640]{2,1,0:T(8,128)(2,1)S(1)}, bf16[2,128,640]{2,1,0:T(8,128)(2,1)S(1)}, u32[]{:S(2)}, u32[]{:S(2)}) collective-permute-start(bf16[2,128,640]{2,1,0:T(8,128)(2,1)S(1)} %get-tuple-element.48), channel_id=1, source_target_pairs={{0,14},{1,15},{2,0},{3,1},{4,2},{5,3},{6,4},{7,5},{8,6},{9,7},{10,... | collective-permute-start | bytes 983048 | tf_op jit(solution)/shard_map/ppermute | solution.py:39
  110.7 22.6 %copy-start.1 = (bf16[1280,1280]{1,0:T(8,128)(2,1)S(1)}, bf16[1280,1280]{1,0:T(8,128)(2,1)}, u32[]{:S(2)}) copy-start(bf16[1280,1280]{1,0:T(8,128)(2,1)} %all-gather.3.cloned.1.call-done.weight.weight0) | copy-start | bytes 9830404
  110.7 22.6 %collective-permute-start.13 = (bf16[2,128,640]{2,1,0:T(8,128)(2,1)}, bf16[2,128,640]{2,1,0:T(8,128)(2,1)}, u32[]{:S(2)}, u32[]{:S(2)}) collective-permute-start(bf16[2,128,640]{2,1,0:T(8,128)(2,1)} %get-tuple-element.49), channel_id=1, source_target_pairs={{0,15},{1,14},{2,1},{3,0},{4,3},{5,2},{6,5},{7,4},{8,7},{9,6},{10,... | collective-permute-start | bytes 983048 | tf_op jit(solution)/shard_map/ppermute | solution.py:39
  111.1 1.6 copy-start.7
  121.1 0.8 copy-start.24
  122.0 0.7 copy-start.28
  122.7 0.7 copy-start.30
  123.4 23.7 %collective-permute-start.11 = (bf16[3,128,640]{2,1,0:T(8,128)(2,1)}, bf16[3,128,640]{2,1,0:T(8,128)(2,1)}, u32[]{:S(2)}, u32[]{:S(2)}) collective-permute-start(bf16[3,128,640]{2,1,0:T(8,128)(2,1)} %get-tuple-element.44), channel_id=1, source_target_pairs={{0,1},{1,0},{2,3},{3,2},{4,5},{5,4},{6,7},{7,6},{8,9},{9,8},{10,11... | collective-permute-start | bytes 1474568 | tf_op jit(solution)/shard_map/ppermute | solution.py:39
  123.6 18.5 %collective-permute-start.15 = (bf16[2,128,640]{2,1,0:T(8,128)(2,1)}, bf16[2,128,640]{2,1,0:T(8,128)(2,1)}, u32[]{:S(2)}, u32[]{:S(2)}) collective-permute-start(bf16[2,128,640]{2,1,0:T(8,128)(2,1)} %get-tuple-element.56), channel_id=1, source_target_pairs={{0,14},{1,15},{2,0},{3,1},{4,2},{5,3},{6,4},{7,5},{8,6},{9,7},{10,... | collective-permute-start | bytes 983048 | tf_op jit(solution)/shard_map/ppermute | solution.py:39
  132.5 0.7 copy-start.15
  133.3 13.8 %collective-permute-start.16 = (bf16[2,128,640]{2,1,0:T(8,128)(2,1)}, bf16[2,128,640]{2,1,0:T(8,128)(2,1)}, u32[]{:S(2)}, u32[]{:S(2)}) collective-permute-start(bf16[2,128,640]{2,1,0:T(8,128)(2,1)} %get-tuple-element.57), channel_id=1, source_target_pairs={{0,15},{1,14},{2,1},{3,0},{4,3},{5,2},{6,5},{7,4},{8,7},{9,6},{10,... | collective-permute-start | bytes 983048 | tf_op jit(solution)/shard_map/ppermute | solution.py:39
  133.3 1.9 %copy-start.2 = (bf16[1280,1280]{1,0:T(8,128)(2,1)S(1)}, bf16[1280,1280]{1,0:T(8,128)(2,1)}, u32[]{:S(2)}) copy-start(bf16[1280,1280]{1,0:T(8,128)(2,1)} %all-gather.5.cloned.1.call-done.weight1) | copy-start | bytes 9830404
  135.2 1.0 copy-start.16
  136.2 1.0 copy-start.27
  137.2 1.0 copy-start.29
  138.1 8.9 %copy-start.17 = (bf16[2,128,640]{2,1,0:T(8,128)(2,1)S(1)}, bf16[2,128,640]{2,1,0:T(8,128)(2,1)}, u32[]{:S(2)}) copy-start(bf16[2,128,640]{2,1,0:T(8,128)(2,1)} %copy-done.15) | copy-start | bytes 983044
  138.1 8.9 %copy-start.23 = (f32[2,128,640]{2,1,0:T(8,128)S(1)}, f32[2,128,640]{2,1,0:T(8,128)}, u32[]{:S(2)}) copy-start(f32[2,128,640]{2,1,0:T(8,128)} %copy-done.22) | copy-start | bytes 1966084
  138.1 8.9 %copy-start.25 = (f32[2,128,640]{2,1,0:T(8,128)S(1)}, f32[2,128,640]{2,1,0:T(8,128)}, u32[]{:S(2)}) copy-start(f32[2,128,640]{2,1,0:T(8,128)} %copy-done.24) | copy-start | bytes 1966084
  141.6 8.3 %collective-permute-start.14 = (bf16[2,128,1280]{2,1,0:T(8,128)(2,1)S(1)}, bf16[2,128,1280]{2,1,0:T(8,128)(2,1)S(1)}, u32[]{:S(2)}, u32[]{:S(2)}) collective-permute-start(bf16[2,128,1280]{2,1,0:T(8,128)(2,1)S(1)} %get-tuple-element.51), channel_id=1, source_target_pairs={{0,1},{1,0},{2,3},{3,2},{4,5},{5,4},{6,7},{7,6},{8,9},{9,8},{10,11... | collective-permute-start | bytes 1966088 | tf_op jit(solution)/shard_map/ppermute | solution.py:39
  147.0 2.8 %copy-start.31 = (bf16[1,128,640]{2,1,0:T(8,128)(2,1)S(1)}, bf16[1,128,640]{2,1,0:T(8,128)(2,1)}, u32[]{:S(2)}) copy-start(bf16[1,128,640]{2,1,0:T(8,128)(2,1)} %copy-done.30) | copy-start | bytes 491524
Sparse Core Ops, SparseCore 0:
  30.0 46.9 all-gather.2
  78.8 44.8 all-gather.4

commit v4 on v3

--- a/solution.py
+++ b/solution.py
@@ -122,29 +122,26 @@
         sib[entry] = source[0, :, columns(3 - 2 * core)]
 
 
-def halves_kernel(place, shard, first, used, other):
+def pass_kernel(rows, first, out):
     del first
-    side = place[1]
-    used[...] = shard[:, columns(side, HALF)]
-    other[...] = shard[:, columns(1 - side, HALF)]
-
-
-def halves(place, shard, first):
+    out[...] = rows[...]
+
+
+def after(rows, first):
     whole = pl.BlockSpec(memory_space=pltpu.VMEM)
-    out = jax.ShapeDtypeStruct((shard.shape[0], HALF), BF16)
-    return pl.pallas_call(
-        halves_kernel,
-        out_shape=(out, out),
-        in_specs=[SCALARS, whole, ANYWHERE],
-        out_specs=(whole, whole),
+    return pl.pallas_call(
+        pass_kernel,
+        out_shape=jax.ShapeDtypeStruct(rows.shape, BF16),
+        in_specs=[whole, ANYWHERE],
+        out_specs=whole,
         compiler_params=pltpu.CompilerParams(vmem_limit_bytes=SMALL_LIMIT),
-        cost_estimate=COST,
-        name="halves",
-    )(place, shard, first)
-
-
-def project_kernel(place, cot, near, pair, pair_near, weight, own, send0, send1, rows):
-    del place
+        cost_estimate=pl.CostEstimate(flops=1, bytes_accessed=1, transcendentals=0),
+        name="after",
+    )(rows, first)
+
+
+def project_kernel(place, cot, near, pair, pair_near, weight, first, own, send0, send1, rows):
+    del place, first
     step = pl.program_id(0)
 
     @pl.when(step == 0)
@@ -164,7 +161,7 @@
             send[...] = out[2 * ROWS :].astype(BF16)
 
 
-def project(place, cot, near, pair, pair_near, weight):
+def project(place, cot, near, pair, pair_near, weight, first):
     def stack(start):
         return pl.BlockSpec((2, ROWS, PART), lambda i, place: (start, 0, 0))
 
@@ -182,6 +179,7 @@
                 stack(0),
                 stack(0),
                 pl.BlockSpec((PART, HALF), lambda i, place: (i, 0)),
+                ANYWHERE,
             ],
             out_specs=(
                 pl.BlockSpec((2 * ROWS, PART), lambda i, place: (0, i)), block, block
@@ -191,7 +189,7 @@
         compiler_params=pltpu.CompilerParams(vmem_limit_bytes=SMALL_LIMIT),
         cost_estimate=COST,
         name="project",
-    )(place, cot, near, pair, pair_near, weight)
+    )(place, cot, near, pair, pair_near, weight, first)
 
 
 def attend_head(core, chunk, head, refs):
@@ -378,25 +376,31 @@
     place = jnp.stack([lax.axis_index("c"), lax.axis_index("x") % 2]).astype(jnp.int32)
     arrays = (q, tq, k, tk, v, tv)
 
-    shard = permute(out_weight, swap_low_and_core)
+    def gathered(shard):
+        return lax.all_gather(shard, "z", axis=0, tiled=True)
+
+    def swapped(half):
+        shard = lax.dynamic_slice_in_dim(out_weight, half * HALF, HALF, axis=1)
+        return permute(shard, swap_low_and_core)
+
+    shard_a, shard_b = swapped(place[1]), swapped(1 - place[1])
+    weight_a = gathered(shard_a)
     own, sib, pair = pack_call(
         pack_first_kernel, "pack_first", [0] * 7, [4, 10, 2], place, *arrays, cot
     )
     near_0 = permute(sib, to_sibling)
     far_a = permute(own, to_chip(1))
     pair = permute(pair, to_pair)
-    weight_a, weight_b = (
-        lax.all_gather(half, "z", axis=0, tiled=True) for half in halves(place, shard, near_0)
-    )
     far, sib = pack_call(
         pack_second_kernel, "pack_second", [0] * 4 + [10], [8, 4], place, k, tk, v, tv, near_0
     )
     near_1 = permute(sib, to_sibling)
     far_b = permute(far, to_chip(1))
     far_c = permute(near_1, to_chip(1))
-    pair_near = permute(pair, to_sibling)
-
-    grad, send_0, send_1 = project(place, cot, near_0, pair, pair_near, weight_a)
+    pair_near = permute(after(pair, far), to_sibling)
+
+    grad, send_0, send_1 = project(place, cot, near_0, pair, pair_near, weight_a, far)
+    weight_b = gathered(shard_b)
     grad_0 = permute(send_0, to_pair)
     grad_1 = permute(send_1, to_pair)
 

time: 160 us -> 157 us (0.981)
  waiting for transfers between devices: 60.4 us -> 46.5 us
  starting transfers between devices: 30.9 us -> 40 us
  local copies, waits for them, and re-layouts: 15.7 us -> 18.8 us
    ppermute x17 -> x18, starting transfers between devices: 30.9 us -> 39.9 us  [permute(): return lax.ppermute(block, AXES, route)]
    all_gather x2, waiting for transfers between devices: 32.6 us -> 23.6 us  [gathered(): return lax.all_gather(shard, 'z', axis=0, tiled=True)]
    ppermute x17 -> x18, waiting for transfers between devices: 27.1 us -> 22.9 us  [permute(): return lax.ppermute(block, AXES, route)]
    unnamed x68 -> x66, local copies, waits for them, and re-layouts: 15.7 us -> 17.6 us
  transfers between devices with their start and end apart: 19 -> 20, of which waited for: 5 -> 7; matrix products, arithmetic and copies ran while one was open for 0% -> 0% of each run, Pallas kernels for 19% -> 22%
where the time goes in v4:
time: 157 us; the launch traced here: 156 us
  waiting for transfers between devices  46.5 us (30%)
  starting transfers between devices  40 us (25%)
  Pallas kernels  36 us (23%)
  local copies, waits for them, and re-layouts  18.8 us (12%)
  between operations  14.3 us (9%)
    ppermute x18, starting transfers between devices, permute(): return lax.ppermute(block, AXES, route)  39.9 us
    all_gather x2, waiting for transfers between devices, gathered(): return lax.all_gather(shard, 'z', axis=0, tiled=True)  23.6 us
    ppermute x18, waiting for transfers between devices, permute(): return lax.ppermute(block, AXES, route)  22.9 us
    unnamed x66, local copies, waits for them, and re-layouts  17.6 us
    pallas_call x2, Pallas kernels, attend(): pl.pallas_call(kernel, out_shape=(out(1, BF16), out(2, F32), out(3, BF16)...  17.3 us
    pallas_call x2, Pallas kernels, pack_call(): pl.pallas_call(kernel, grid=(steps,), out_shape=[stacked(n) for n in outp...  6.82 us
    pallas_call x2, Pallas kernels, finish(): pl.pallas_call(kernel, out_shape=(out, out), in_specs=[SCALARS] + [whole]...  5.17 us
    pallas_call x1, Pallas kernels, tangent(): pl.pallas_call(tangent_kernel, out_shape=(jax.ShapeDtypeStruct((2, ROWS,...  3.41 us
  transfers between devices with their start and end apart: 20, of which 7 were waited for; matrix products, arithmetic and copies ran while one was open for 0% of the time, Pallas kernels for 22%

profile of v4, /device:TPU:1, one launch (start us, length us, event | category | flops | bytes accessed | tf_op | source)
XLA Modules:
  0.0 156.2 jit_solution(15062922212062337005)
XLA Ops:
  7.2 0.0 all-gather.3.cloned.1.call-start
  7.2 1.2 constant_dynamic-slice_fusion
  8.4 4.6 %collective-permute-start.5 = (bf16[160,1280]{1,0:T(8,128)(2,1)S(1)}, bf16[160,1280]{1,0:T(8,128)(2,1)S(1)}, u32[]{:S(2)}, u32[]{:S(2)}) collective-permute-start(bf16[160,1280]{1,0:T(8,128)(2,1)S(1)} %get-tuple-element.57), channel_id=1, source_target_pairs={{0,0},{1,128},{2,2},{3,130},{4,4},{5,132},{6,6},{7,134},{8,8},{9,1... | collective-permute-start | bytes 1228808 | tf_op jit(solution)/shard_map/ppermute | solution.py:39
  13.0 5.6 %collective-permute-done.5 = bf16[160,1280]{1,0:T(8,128)(2,1)S(1)} collective-permute-done((bf16[160,1280]{1,0:T(8,128)(2,1)S(1)}, bf16[160,1280]{1,0:T(8,128)(2,1)S(1)}, u32[]{:S(2)}, u32[]{:S(2)}) %collective-permute-start.5) | collective-permute-done | bytes 409632 | tf_op jit(solution)/shard_map/ppermute | solution.py:39
  18.6 0.7 copy-done.32
  19.4 0.0 all-gather.3.cloned.1.call-update
  19.4 0.0 all-gather.5.cloned.1.call-start
  19.5 3.6 %collective-permute-start.12 = (bf16[160,1280]{1,0:T(8,128)(2,1)S(1)}, bf16[160,1280]{1,0:T(8,128)(2,1)S(1)}, u32[]{:S(2)}, u32[]{:S(2)}) collective-permute-start(bf16[160,1280]{1,0:T(8,128)(2,1)S(1)} %get-tuple-element.56), channel_id=1, source_target_pairs={{0,0},{1,128},{2,2},{3,130},{4,4},{5,132},{6,6},{7,134},{8,8},{9,1... | collective-permute-start | bytes 1228808 | tf_op jit(solution)/shard_map/ppermute | solution.py:39
  23.1 0.6 pad_add_fusion.place
  23.7 3.4 %pack_first.1 = (bf16[4,128,640]{2,1,0:T(8,128)(2,1)}, bf16[10,128,640]{2,1,0:T(8,128)(2,1)}, bf16[2,128,640]{2,1,0:T(8,128)(2,1)}) custom-call(s32[2]{0:T(128)} %pad_add_fusion.place, bf16[1,128,2560]{2,1,0:T(8,128)(2,1)} %refs_0_.3, bf16[1,128,2560]{2,1,0:T(8,128)(2,1)} %refs_1_.3, bf16[1,128,2560]{2,1,0:T(8,128)(2,1)} %refs_2_.3, ...), custom_call_target="tpu_custom_call" | custom-call | flops 10000000000 | bytes 10000000 | tf_op jit(solution)/shard_map/pack_first/pallas_call | solution.py:92
  27.2 0.0 collective-permute-start
  27.2 1.5 collective-permute-done.12
  28.7 0.8 copy-done.31
  29.5 0.0 all-gather.5.cloned.1.call-update
  29.5 1.3 collective-permute-start.3
  30.8 0.1 collective-permute-done.near.refs_6_.refs_7_
  30.9 1.3 copy-done.3
  32.2 3.4 %pack_second.1 = (bf16[8,128,640]{2,1,0:T(8,128)(2,1)}, bf16[4,128,640]{2,1,0:T(8,128)(2,1)}) custom-call(s32[2]{0:T(128)} %pad_add_fusion.place, bf16[1,128,2560]{2,1,0:T(8,128)(2,1)} %refs_2_.3, bf16[1,128,2560]{2,1,0:T(8,128)(2,1)} %refs_3_.3, bf16[1,128,2560]{2,1,0:T(8,128)(2,1)} %refs_4_.3, bf16[1,128,2560]{2,1,0:T(8,128)(2,1)} %refs_5_.3, ...), custom_call_target="tpu_custom_call" | custom-call | flops 10000000000 | bytes 10000000 | tf_op jit(solution)/shard_map/pack_second/pallas_call | solution.py:92
  35.5 3.5 %collective-permute-done.3.rows.pair = bf16[2,128,640]{2,1,0:T(8,128)(2,1)S(1)} collective-permute-done((bf16[2,128,640]{2,1,0:T(8,128)(2,1)}, bf16[2,128,640]{2,1,0:T(8,128)(2,1)S(1)}, u32[]{:S(2)}, u32[]{:S(2)}) %collective-permute-start.3) | collective-permute-done | bytes 327712 | tf_op jit(solution)/shard_map/ppermute | solution.py:39
  39.1 0.1 collective-permute-start.4
  39.2 2.7 %collective-permute-start.2 = (bf16[8,128,640]{2,1,0:T(8,128)(2,1)}, bf16[8,128,640]{2,1,0:T(8,128)(2,1)S(1)}, u32[]{:S(2)}, u32[]{:S(2)}) collective-permute-start(bf16[8,128,640]{2,1,0:T(8,128)(2,1)} %get-tuple-element.32.first), channel_id=1, source_target_pairs={{0,2},{1,3},{2,4},{3,5},{4,6},{5,7},{6,8},{7,9},{8,10},{9,11},{10,... | collective-permute-start | bytes 3932168 | tf_op jit(solution)/shard_map/ppermute | solution.py:39
  41.9 1.3 collective-permute-start.1
  43.2 1.0 collective-permute-start.7
  44.2 0.0 collective-permute-done.4.pair_near
  44.2 0.7 copy-done.18
  44.9 23.6 %all-gather.3.cloned.1.call-done.weight.weight0 = bf16[1280,1280]{1,0:T(8,128)(2,1)} async-done(((bf16[160,1280]{1,0:T(8,128)(2,1)}), bf16[1280,1280]{1,0:T(8,128)(2,1)}) %all-gather.3.cloned.1.call-update) | async-done | bytes 3276816 | tf_op jit(solution)/shard_map/all_gather | solution.py:380
  68.5 1.9 %copy-done = bf16[1280,1280]{1,0:T(8,128)(2,1)S(1)} copy-done((bf16[1280,1280]{1,0:T(8,128)(2,1)S(1)}, bf16[1280,1280]{1,0:T(8,128)(2,1)}, u32[]{:S(2)}) %copy-start) | copy-done | bytes 3276824
  70.4 1.1 copy-done.8
  71.5 1.0 copy-done.19
  72.5 0.0 copy-start.13
  72.5 0.0 copy-start.14
  72.5 3.3 %project.1 = (f32[256,1280]{1,0:T(8,128)S(1)}, bf16[256,640]{1,0:T(8,128)(2,1)S(1)}, bf16[256,640]{1,0:T(8,128)(2,1)S(1)}) custom-call(s32[2]{0:T(128)S(1)} %copy-done.20, bf16[1,128,2560]{2,1,0:T(8,128)(2,1)S(1)} %copy-done.8, bf16[10,128,640]{2,1,0:T(8,128)(2,1)S(1)} %copy-done.4, bf16[2,128,640]{2,1,0:T(8,128)(2,1)S(1)} %collective-permute-done.3.rows.pair, ...), custom_call_target="tpu_custom_call" | custom-call | flops 10000000000 | bytes 10000000 | tf_op jit(solution)/shard_map/project/pallas_call | solution.py:170
  75.8 1.3 collective-permute-start.6
  77.1 2.7 %collective-permute-start.8 = (bf16[4,128,640]{2,1,0:T(8,128)(2,1)}, bf16[4,128,640]{2,1,0:T(8,128)(2,1)S(1)}, u32[]{:S(2)}, u32[]{:S(2)}) collective-permute-start(bf16[4,128,640]{2,1,0:T(8,128)(2,1)} %collective-permute-done.7.refs_6_), channel_id=1, source_target_pairs={{0,2},{1,3},{2,4},{3,5},{4,6},{5,7},{6,8},{7,9},{8,10},{9,11},{10,... | collective-permute-start | bytes 1966088 | tf_op jit(solution)/shard_map/ppermute | solution.py:39
  79.8 0.3 collective-permute-start.9
  80.1 7.1 %collective-permute-done.1.refs_8_ = bf16[4,128,640]{2,1,0:T(8,128)(2,1)} collective-permute-done((bf16[4,128,640]{2,1,0:T(8,128)(2,1)}, bf16[4,128,640]{2,1,0:T(8,128)(2,1)}, u32[]{:S(2)}, u32[]{:S(2)}) %collective-permute-start.1) | collective-permute-done | bytes 655392 | tf_op jit(solution)/shard_map/ppermute | solution.py:39
  87.3 8.8 %attend.2 = (bf16[1,128,640]{2,1,0:T(8,128)(2,1)S(1)}, f32[2,128,640]{2,1,0:T(8,128)S(1)}, bf16[3,128,640]{2,1,0:T(8,128)(2,1)}, bf16[2,128,640]{2,1,0:T(8,128)(...) custom-call(s32[2]{0:T(128)S(1)} %copy-done.20, bf16[1,128,2560]{2,1,0:T(8,128)(2,1)S(1)} %copy-done.9, ...), custom_call_target="tpu_custom_call" | custom-call | flops 10000000000 | bytes 10000000 | tf_op jit(solution)/shard_map/attend/pallas_call | solution.py:277
  96.1 0.8 copy-done.21
  96.9 2.1 %collective-permute-start.10 = (bf16[3,128,640]{2,1,0:T(8,128)(2,1)}, bf16[3,128,640]{2,1,0:T(8,128)(2,1)}, u32[]{:S(2)}, u32[]{:S(2)}) collective-permute-start(bf16[3,128,640]{2,1,0:T(8,128)(2,1)} %get-tuple-element.40), channel_id=1, source_target_pairs={{0,1},{1,0},{2,3},{3,2},{4,5},{5,4},{6,7},{7,6},{8,9},{9,8},{10,11... | collective-permute-start | bytes 1474568 | tf_op jit(solution)/shard_map/ppermute | solution.py:39
  99.0 7.9 %collective-permute-start.13 = (bf16[2,128,640]{2,1,0:T(8,128)(2,1)S(1)}, bf16[2,128,640]{2,1,0:T(8,128)(2,1)S(1)}, u32[]{:S(2)}, u32[]{:S(2)}) collective-permute-start(bf16[2,128,640]{2,1,0:T(8,128)(2,1)S(1)} %get-tuple-element.44), channel_id=1, source_target_pairs={{0,14},{1,15},{2,0},{3,1},{4,2},{5,3},{6,4},{7,5},{8,6},{9,7},{10,... | collective-permute-start | bytes 983048 | tf_op jit(solution)/shard_map/ppermute | solution.py:39
  106.9 0.0 collective-permute-start.14
  106.9 0.0 collective-permute-done.8.refs_9_
  106.9 1.5 copy-done.7
  108.4 8.5 %attend.3 = (bf16[1,128,640]{2,1,0:T(8,128)(2,1)S(1)}, f32[2,128,640]{2,1,0:T(8,128)S(1)}, bf16[3,128,640]{2,1,0:T(8,128)(2,1)}, bf16[2,128,640]{2,1,0:T(8,128)(...) custom-call(s32[2]{0:T(128)S(1)} %copy-done.20, bf16[1,128,2560]{2,1,0:T(8,128)(2,1)S(1)} %copy-done.9, ...), custom_call_target="tpu_custom_call" | custom-call | flops 10000000000 | bytes 10000000 | tf_op jit(solution)/shard_map/attend/pallas_call | solution.py:277
  116.9 0.8 copy-done.23
  117.7 0.7 copy-done.27
  118.4 0.6 copy-done.29
  119.1 0.4 collective-permute-start.11
  119.5 10.3 %collective-permute-start.16 = (bf16[2,128,640]{2,1,0:T(8,128)(2,1)}, bf16[2,128,640]{2,1,0:T(8,128)(2,1)}, u32[]{:S(2)}, u32[]{:S(2)}) collective-permute-start(bf16[2,128,640]{2,1,0:T(8,128)(2,1)} %get-tuple-element.52), channel_id=1, source_target_pairs={{0,14},{1,15},{2,0},{3,1},{4,2},{5,3},{6,4},{7,5},{8,6},{9,7},{10,... | collective-permute-start | bytes 983048 | tf_op jit(solution)/shard_map/ppermute | solution.py:39
  129.7 0.0 collective-permute-done.13.back.near0
  129.7 0.7 copy-done.15
  130.4 0.0 collective-permute-start.17
  130.5 0.0 collective-permute-done.10.near.sib0
  130.5 1.9 %copy-done.2 = bf16[1280,1280]{1,0:T(8,128)(2,1)S(1)} copy-done((bf16[1280,1280]{1,0:T(8,128)(2,1)S(1)}, bf16[1280,1280]{1,0:T(8,128)(2,1)}, u32[]{:S(2)}) %copy-start.2) | copy-done | bytes 3276824
  132.4 1.0 copy-done.16
  133.4 1.0 copy-done.26
  134.4 1.0 copy-done.28
  135.3 3.4 %tangent.1 = (f32[2,128,1280]{2,1,0:T(8,128)S(1)}, bf16[2,128,1280]{2,1,0:T(8,128)(2,1)S(1)}) custom-call(s32[2]{0:T(128)S(1)} %copy-done.20, bf16[256,640]{1,0:T(8,128)(2,1)S(1)} %copy-done.26, bf16[256,640]{1,0:T(8,128)(2,1)S(1)} %copy-done.28, bf16[1280,1280]{1,0:T(8,128)(2,1)S(1)} %copy-done.1, bf16[1280,1280]{1,0:T(8,128)(2,1)S(1)} %copy-done.2, ...), custom_call_target="tpu_custom_call" | custom-call | flops 10000000000 | bytes 10000000 | tf_op jit(solution)/shard_map/tangent/pallas_call | solution.py:310
  138.8 0.5 collective-permute-start.15
  139.2 0.0 collective-permute-done.16.near1
  139.2 5.0 %collective-permute-done.17.cross1 = bf16[2,128,640]{2,1,0:T(8,128)(2,1)} collective-permute-done((bf16[2,128,640]{2,1,0:T(8,128)(2,1)}, bf16[2,128,640]{2,1,0:T(8,128)(2,1)}, u32[]{:S(2)}, u32[]{:S(2)}) %collective-permute-start.17) | collective-permute-done | bytes 327712 | tf_op jit(solution)/shard_map/ppermute | solution.py:39
  144.2 2.8 %finish_last.1 = (bf16[1,128,2560]{2,1,0:T(8,128)(2,1)}, bf16[1,128,2560]{2,1,0:T(8,128)(2,1)}) custom-call(s32[2]{0:T(128)S(1)} %copy-done.20, f32[2,128,640]{2,1,0:T(8,128)S(1)} %copy-done.22, f32[2,128,640]{2,1,0:T(8,128)S(1)} %copy-done.24, bf16[3,128,640]{2,1,0:T(8,128)(2,1)} %collective-permute-done.10.near.sib0, ...), custom_call_target="tpu_custom_call" | custom-call | flops 10000000000 | bytes 10000000 | tf_op jit(solution)/shard_map/finish_last/pallas_call | solution.py:364
  147.0 0.0 collective-permute-done.15.tan_sib
  147.0 2.4 %finish_first.1 = (bf16[1,128,2560]{2,1,0:T(8,128)(2,1)}, bf16[1,128,2560]{2,1,0:T(8,128)(2,1)}) custom-call(s32[2]{0:T(128)S(1)} %copy-done.20, bf16[1,128,640]{2,1,0:T(8,128)(2,1)S(1)} %get-tuple-element.36.own0, bf16[1,128,640]{2,1,0:T(8,128)(2,1)S(1)} %copy-done.30, bf16[3,128,640]{2,1,0:T(8,128)(2,1)} %collective-permute-done.10.near.sib0, ...), custom_call_target="tpu_custom_call" | custom-call | flops 10000000000 | bytes 10000000 | tf_op jit(solution)/shard_map/finish_first/pallas_call | solution.py:364
  (55 shorter events, 0.1 us)
Async XLA Ops:
  7.2 61.3 %all-gather.3.cloned.1.call-start = ((), (), s32[]{:S(2)}) async-start(), calls=%async_computation | async-start | bytes 3686400 | tf_op jit(solution)/shard_map/all_gather | solution.py:380
  8.4 10.2 %collective-permute-start.5 = (bf16[160,1280]{1,0:T(8,128)(2,1)S(1)}, bf16[160,1280]{1,0:T(8,128)(2,1)S(1)}, u32[]{:S(2)}, u32[]{:S(2)}) collective-permute-start(bf16[160,1280]{1,0:T(8,128)(2,1)S(1)} %get-tuple-element.57), channel_id=1, source_target_pairs={{0,0},{1,128},{2,2},{3,130},{4,4},{5,132},{6,6},{7,134},{8,8},{9,1... | collective-permute-start | bytes 1228808 | tf_op jit(solution)/shard_map/ppermute | solution.py:39
  18.6 0.8 copy-start.32
  19.4 111.0 %all-gather.5.cloned.1.call-start = ((), (), s32[]{:S(2)}) async-start(), calls=%async_computation.1 | async-start | bytes 3686400 | tf_op jit(solution)/shard_map/all_gather | solution.py:380
  19.5 9.3 %collective-permute-start.12 = (bf16[160,1280]{1,0:T(8,128)(2,1)S(1)}, bf16[160,1280]{1,0:T(8,128)(2,1)S(1)}, u32[]{:S(2)}, u32[]{:S(2)}) collective-permute-start(bf16[160,1280]{1,0:T(8,128)(2,1)S(1)} %get-tuple-element.56), channel_id=1, source_target_pairs={{0,0},{1,128},{2,2},{3,130},{4,4},{5,132},{6,6},{7,134},{8,8},{9,1... | collective-permute-start | bytes 1228808 | tf_op jit(solution)/shard_map/ppermute | solution.py:39
  27.2 3.7 %collective-permute-start = (bf16[10,128,640]{2,1,0:T(8,128)(2,1)}, bf16[10,128,640]{2,1,0:T(8,128)(2,1)S(1)}, u32[]{:S(2)}, u32[]{:S(2)}) collective-permute-start(bf16[10,128,640]{2,1,0:T(8,128)(2,1)} %get-tuple-element.30), channel_id=1, source_target_pairs={{0,1},{1,0},{2,3},{3,2},{4,5},{5,4},{6,7},{7,6},{8,9},{9,8},{10,11... | collective-permute-start | bytes 4915208 | tf_op jit(solution)/shard_map/ppermute | solution.py:39
  28.7 0.8 copy-start.31
  29.5 9.6 %collective-permute-start.3 = (bf16[2,128,640]{2,1,0:T(8,128)(2,1)}, bf16[2,128,640]{2,1,0:T(8,128)(2,1)S(1)}, u32[]{:S(2)}, u32[]{:S(2)}) collective-permute-start(bf16[2,128,640]{2,1,0:T(8,128)(2,1)} %get-tuple-element.33), channel_id=1, source_target_pairs={{0,4},{1,5},{2,6},{3,7},{4,0},{5,1},{6,2},{7,3},{8,12},{9,13},{10,... | collective-permute-start | bytes 983048 | tf_op jit(solution)/shard_map/ppermute | solution.py:39
  30.9 1.3 copy-start.3
  35.5 32.9 %copy-start.4 = (bf16[10,128,640]{2,1,0:T(8,128)(2,1)S(1)}, bf16[10,128,640]{2,1,0:T(8,128)(2,1)}, u32[]{:S(2)}) copy-start(bf16[10,128,640]{2,1,0:T(8,128)(2,1)} %copy-done.3) | copy-start | bytes 4915204
  35.5 32.9 %copy-start.20 = (s32[2]{0:T(128)S(1)}, s32[2]{0:T(128)}, u32[]{:S(2)}) copy-start(s32[2]{0:T(128)} %pad_add_fusion.place) | copy-start | bytes 28
  39.1 5.1 %collective-permute-start.4 = (bf16[2,128,640]{2,1,0:T(8,128)(2,1)S(1)}, bf16[2,128,640]{2,1,0:T(8,128)(2,1)S(1)}, u32[]{:S(2)}, u32[]{:S(2)}) collective-permute-start(bf16[2,128,640]{2,1,0:T(8,128)(2,1)S(1)} %after.1), channel_id=1, source_target_pairs={{0,1},{1,0},{2,3},{3,2},{4,5},{5,4},{6,7},{7,6},{8,9},{9,8},{10,11... | collective-permute-start | bytes 983048 | tf_op jit(solution)/shard_map/ppermute | solution.py:39
  39.2 48.0 %collective-permute-start.2 = (bf16[8,128,640]{2,1,0:T(8,128)(2,1)}, bf16[8,128,640]{2,1,0:T(8,128)(2,1)S(1)}, u32[]{:S(2)}, u32[]{:S(2)}) collective-permute-start(bf16[8,128,640]{2,1,0:T(8,128)(2,1)} %get-tuple-element.32.first), channel_id=1, source_target_pairs={{0,2},{1,3},{2,4},{3,5},{4,6},{5,7},{6,8},{7,9},{8,10},{9,11},{10,... | collective-permute-start | bytes 3932168 | tf_op jit(solution)/shard_map/ppermute | solution.py:39
  41.9 45.3 %collective-permute-start.1 = (bf16[4,128,640]{2,1,0:T(8,128)(2,1)}, bf16[4,128,640]{2,1,0:T(8,128)(2,1)}, u32[]{:S(2)}, u32[]{:S(2)}) collective-permute-start(bf16[4,128,640]{2,1,0:T(8,128)(2,1)} %get-tuple-element.31), channel_id=1, source_target_pairs={{0,2},{1,3},{2,4},{3,5},{4,6},{5,7},{6,8},{7,9},{8,10},{9,11},{10,... | collective-permute-start | bytes 1966088 | tf_op jit(solution)/shard_map/ppermute | solution.py:39
  43.2 33.9 %collective-permute-start.7 = (bf16[4,128,640]{2,1,0:T(8,128)(2,1)}, bf16[4,128,640]{2,1,0:T(8,128)(2,1)}, u32[]{:S(2)}, u32[]{:S(2)}) collective-permute-start(bf16[4,128,640]{2,1,0:T(8,128)(2,1)} %get-tuple-element.37), channel_id=1, source_target_pairs={{0,1},{1,0},{2,3},{3,2},{4,5},{5,4},{6,7},{7,6},{8,9},{9,8},{10,11... | collective-permute-start | bytes 1966088 | tf_op jit(solution)/shard_map/ppermute | solution.py:39
  44.2 0.7 copy-start.18
  68.5 1.9 %copy-start = (bf16[1280,1280]{1,0:T(8,128)(2,1)S(1)}, bf16[1280,1280]{1,0:T(8,128)(2,1)}, u32[]{:S(2)}) copy-start(bf16[1280,1280]{1,0:T(8,128)(2,1)} %all-gather.3.cloned.1.call-done.weight.weight0) | copy-start | bytes 9830404
  70.4 1.1 copy-start.8
  71.5 1.0 copy-start.19
  72.5 14.8 %copy-start.9 = (bf16[1,128,2560]{2,1,0:T(8,128)(2,1)S(1)}, bf16[1,128,2560]{2,1,0:T(8,128)(2,1)}, u32[]{:S(2)}) copy-start(bf16[1,128,2560]{2,1,0:T(8,128)(2,1)} %refs_0_.3) | copy-start | bytes 1966084
  72.5 14.8 %copy-start.10 = (bf16[1,128,2560]{2,1,0:T(8,128)(2,1)S(1)}, bf16[1,128,2560]{2,1,0:T(8,128)(2,1)}, u32[]{:S(2)}) copy-start(bf16[1,128,2560]{2,1,0:T(8,128)(2,1)} %refs_1_.3) | copy-start | bytes 1966084
  72.5 14.8 %copy-start.11 = (bf16[1,128,2560]{2,1,0:T(8,128)(2,1)S(1)}, bf16[1,128,2560]{2,1,0:T(8,128)(2,1)}, u32[]{:S(2)}) copy-start(bf16[1,128,2560]{2,1,0:T(8,128)(2,1)} %refs_2_.3) | copy-start | bytes 1966084
  72.5 14.8 %copy-start.12 = (bf16[1,128,2560]{2,1,0:T(8,128)(2,1)S(1)}, bf16[1,128,2560]{2,1,0:T(8,128)(2,1)}, u32[]{:S(2)}) copy-start(bf16[1,128,2560]{2,1,0:T(8,128)(2,1)} %refs_3_.3) | copy-start | bytes 1966084
  72.5 14.8 %copy-start.13 = (bf16[1,128,2560]{2,1,0:T(8,128)(2,1)S(1)}, bf16[1,128,2560]{2,1,0:T(8,128)(2,1)}, u32[]{:S(2)}) copy-start(bf16[1,128,2560]{2,1,0:T(8,128)(2,1)} %refs_4_.3) | copy-start | bytes 1966084
  72.5 14.8 %copy-start.14 = (bf16[1,128,2560]{2,1,0:T(8,128)(2,1)S(1)}, bf16[1,128,2560]{2,1,0:T(8,128)(2,1)}, u32[]{:S(2)}) copy-start(bf16[1,128,2560]{2,1,0:T(8,128)(2,1)} %refs_5_.3) | copy-start | bytes 1966084
  75.8 11.4 %collective-permute-start.6 = (bf16[256,640]{1,0:T(8,128)(2,1)S(1)}, bf16[256,640]{1,0:T(8,128)(2,1)S(1)}, u32[]{:S(2)}, u32[]{:S(2)}) collective-permute-start(bf16[256,640]{1,0:T(8,128)(2,1)S(1)} %get-tuple-element.35), channel_id=1, source_target_pairs={{0,4},{1,5},{2,6},{3,7},{4,0},{5,1},{6,2},{7,3},{8,12},{9,13},{10,... | collective-permute-start | bytes 983048 | tf_op jit(solution)/shard_map/ppermute | solution.py:39
  77.1 29.8 %collective-permute-start.8 = (bf16[4,128,640]{2,1,0:T(8,128)(2,1)}, bf16[4,128,640]{2,1,0:T(8,128)(2,1)S(1)}, u32[]{:S(2)}, u32[]{:S(2)}) collective-permute-start(bf16[4,128,640]{2,1,0:T(8,128)(2,1)} %collective-permute-done.7.refs_6_), channel_id=1, source_target_pairs={{0,2},{1,3},{2,4},{3,5},{4,6},{5,7},{6,8},{7,9},{8,10},{9,11},{10,... | collective-permute-start | bytes 1966088 | tf_op jit(solution)/shard_map/ppermute | solution.py:39
  79.8 27.1 %collective-permute-start.9 = (bf16[256,640]{1,0:T(8,128)(2,1)S(1)}, bf16[256,640]{1,0:T(8,128)(2,1)S(1)}, u32[]{:S(2)}, u32[]{:S(2)}) collective-permute-start(bf16[256,640]{1,0:T(8,128)(2,1)S(1)} %get-tuple-element.38), channel_id=1, source_target_pairs={{0,4},{1,5},{2,6},{3,7},{4,0},{5,1},{6,2},{7,3},{8,12},{9,13},{10,... | collective-permute-start | bytes 983048 | tf_op jit(solution)/shard_map/ppermute | solution.py:39
  87.2 8.9 %copy-start.6 = (bf16[8,128,640]{2,1,0:T(8,128)(2,1)}, bf16[8,128,640]{2,1,0:T(8,128)(2,1)S(1)}, u32[]{:S(2)}) copy-start(bf16[8,128,640]{2,1,0:T(8,128)(2,1)S(1)} %collective-permute-done.2.refs_9_.refs_8_) | copy-start | bytes 3932164
  87.3 19.6 %copy-start.5 = (bf16[10,128,640]{2,1,0:T(8,128)(2,1)S(1)}, bf16[10,128,640]{2,1,0:T(8,128)(2,1)}, u32[]{:S(2)}) copy-start(bf16[10,128,640]{2,1,0:T(8,128)(2,1)} %copy-done.3) | copy-start | bytes 4915204
  96.1 0.8 copy-start.21
  96.9 19.9 %copy-start.25 = (bf16[256,640]{1,0:T(8,128)(2,1)}, bf16[256,640]{1,0:T(8,128)(2,1)S(1)}, u32[]{:S(2)}) copy-start(bf16[256,640]{1,0:T(8,128)(2,1)S(1)} %get-tuple-element.42.tan0) | copy-start | bytes 983044
  96.9 33.5 %collective-permute-start.10 = (bf16[3,128,640]{2,1,0:T(8,128)(2,1)}, bf16[3,128,640]{2,1,0:T(8,128)(2,1)}, u32[]{:S(2)}, u32[]{:S(2)}) collective-permute-start(bf16[3,128,640]{2,1,0:T(8,128)(2,1)} %get-tuple-element.40), channel_id=1, source_target_pairs={{0,1},{1,0},{2,3},{3,2},{4,5},{5,4},{6,7},{7,6},{8,9},{9,8},{10,11... | collective-permute-start | bytes 1474568 | tf_op jit(solution)/shard_map/ppermute | solution.py:39
  99.0 30.7 %collective-permute-start.13 = (bf16[2,128,640]{2,1,0:T(8,128)(2,1)S(1)}, bf16[2,128,640]{2,1,0:T(8,128)(2,1)S(1)}, u32[]{:S(2)}, u32[]{:S(2)}) collective-permute-start(bf16[2,128,640]{2,1,0:T(8,128)(2,1)S(1)} %get-tuple-element.44), channel_id=1, source_target_pairs={{0,14},{1,15},{2,0},{3,1},{4,2},{5,3},{6,4},{7,5},{8,6},{9,7},{10,... | collective-permute-start | bytes 983048 | tf_op jit(solution)/shard_map/ppermute | solution.py:39
  106.9 23.6 %copy-start.1 = (bf16[1280,1280]{1,0:T(8,128)(2,1)S(1)}, bf16[1280,1280]{1,0:T(8,128)(2,1)}, u32[]{:S(2)}) copy-start(bf16[1280,1280]{1,0:T(8,128)(2,1)} %all-gather.3.cloned.1.call-done.weight.weight0) | copy-start | bytes 9830404
  106.9 23.6 %collective-permute-start.14 = (bf16[2,128,640]{2,1,0:T(8,128)(2,1)}, bf16[2,128,640]{2,1,0:T(8,128)(2,1)}, u32[]{:S(2)}, u32[]{:S(2)}) collective-permute-start(bf16[2,128,640]{2,1,0:T(8,128)(2,1)} %get-tuple-element.45), channel_id=1, source_target_pairs={{0,15},{1,14},{2,1},{3,0},{4,3},{5,2},{6,5},{7,4},{8,7},{9,6},{10,... | collective-permute-start | bytes 983048 | tf_op jit(solution)/shard_map/ppermute | solution.py:39
  106.9 1.5 copy-start.7
  116.9 0.8 copy-start.23
  117.7 0.7 copy-start.27
  118.4 0.7 copy-start.29
  119.1 25.1 %collective-permute-start.11 = (bf16[3,128,640]{2,1,0:T(8,128)(2,1)}, bf16[3,128,640]{2,1,0:T(8,128)(2,1)}, u32[]{:S(2)}, u32[]{:S(2)}) collective-permute-start(bf16[3,128,640]{2,1,0:T(8,128)(2,1)} %get-tuple-element.41), channel_id=1, source_target_pairs={{0,1},{1,0},{2,3},{3,2},{4,5},{5,4},{6,7},{7,6},{8,9},{9,8},{10,11... | collective-permute-start | bytes 1474568 | tf_op jit(solution)/shard_map/ppermute | solution.py:39
  119.5 19.8 %collective-permute-start.16 = (bf16[2,128,640]{2,1,0:T(8,128)(2,1)}, bf16[2,128,640]{2,1,0:T(8,128)(2,1)}, u32[]{:S(2)}, u32[]{:S(2)}) collective-permute-start(bf16[2,128,640]{2,1,0:T(8,128)(2,1)} %get-tuple-element.52), channel_id=1, source_target_pairs={{0,14},{1,15},{2,0},{3,1},{4,2},{5,3},{6,4},{7,5},{8,6},{9,7},{10,... | collective-permute-start | bytes 983048 | tf_op jit(solution)/shard_map/ppermute | solution.py:39
  129.7 0.7 copy-start.15
  130.4 13.8 %collective-permute-start.17 = (bf16[2,128,640]{2,1,0:T(8,128)(2,1)}, bf16[2,128,640]{2,1,0:T(8,128)(2,1)}, u32[]{:S(2)}, u32[]{:S(2)}) collective-permute-start(bf16[2,128,640]{2,1,0:T(8,128)(2,1)} %get-tuple-element.53), channel_id=1, source_target_pairs={{0,15},{1,14},{2,1},{3,0},{4,3},{5,2},{6,5},{7,4},{8,7},{9,6},{10,... | collective-permute-start | bytes 983048 | tf_op jit(solution)/shard_map/ppermute | solution.py:39
  130.5 1.9 %copy-start.2 = (bf16[1280,1280]{1,0:T(8,128)(2,1)S(1)}, bf16[1280,1280]{1,0:T(8,128)(2,1)}, u32[]{:S(2)}) copy-start(bf16[1280,1280]{1,0:T(8,128)(2,1)} %all-gather.5.cloned.1.call-done.weight1) | copy-start | bytes 9830404
  132.4 1.0 copy-start.16
  133.4 1.0 copy-start.26
  134.4 1.0 copy-start.28
  135.3 8.9 %copy-start.17 = (bf16[2,128,640]{2,1,0:T(8,128)(2,1)S(1)}, bf16[2,128,640]{2,1,0:T(8,128)(2,1)}, u32[]{:S(2)}) copy-start(bf16[2,128,640]{2,1,0:T(8,128)(2,1)} %copy-done.15) | copy-start | bytes 983044
  135.3 8.9 %copy-start.22 = (f32[2,128,640]{2,1,0:T(8,128)S(1)}, f32[2,128,640]{2,1,0:T(8,128)}, u32[]{:S(2)}) copy-start(f32[2,128,640]{2,1,0:T(8,128)} %copy-done.21) | copy-start | bytes 1966084
  135.3 8.9 %copy-start.24 = (f32[2,128,640]{2,1,0:T(8,128)S(1)}, f32[2,128,640]{2,1,0:T(8,128)}, u32[]{:S(2)}) copy-start(f32[2,128,640]{2,1,0:T(8,128)} %copy-done.23) | copy-start | bytes 1966084
  138.8 8.3 %collective-permute-start.15 = (bf16[2,128,1280]{2,1,0:T(8,128)(2,1)S(1)}, bf16[2,128,1280]{2,1,0:T(8,128)(2,1)S(1)}, u32[]{:S(2)}, u32[]{:S(2)}) collective-permute-start(bf16[2,128,1280]{2,1,0:T(8,128)(2,1)S(1)} %get-tuple-element.47), channel_id=1, source_target_pairs={{0,1},{1,0},{2,3},{3,2},{4,5},{5,4},{6,7},{7,6},{8,9},{9,8},{10,11... | collective-permute-start | bytes 1966088 | tf_op jit(solution)/shard_map/ppermute | solution.py:39
  144.2 2.8 %copy-start.30 = (bf16[1,128,640]{2,1,0:T(8,128)(2,1)S(1)}, bf16[1,128,640]{2,1,0:T(8,128)(2,1)}, u32[]{:S(2)}) copy-start(bf16[1,128,640]{2,1,0:T(8,128)(2,1)} %copy-done.29) | copy-start | bytes 491524
Sparse Core Ops, SparseCore 0:
  19.5 48.8 all-gather.2
  70.2 44.8 all-gather.4
